TPU v7x, 512 devices: a whole 4x4x16 slice. The times are simulated.
512 devices in a mesh: tm: 64 (over x, y, z_lo), head: 8 (over z_hi, core).
Axes of the slice: x: 4, y: 4, z: 16 (z_hi: 4, z_lo: 4; z = z_hi * 4 + z_lo), core: 2. Of those that a mesh axis runs over, the one named last changes fastest.
Arguments:
- query: bfloat16 [32768, 5120], P('tm', 'head'), may hold values from -100 to 100
- key: bfloat16 [32768, 5120], P('tm', 'head'), may hold values from -100 to 100
- value: bfloat16 [32768, 5120], P('tm', 'head'), may hold values from -6 to 6
- q_gain: float32 [5120], P('head'), may hold values from 0.1 to 1.9
- k_gain: float32 [5120], P('head'), may hold values from 0.1 to 1.9
- far_frames: int32 [512, 12], replicated, may hold values from -1 to 63, as said below
- far_pick: int32 [64, 64], replicated, may hold values from 0 to 7
Outputs:
- attended: bfloat16 [32768, 5120], P('tm', 'head')
Inputs may be any that keep to these rules, and one draw needn't show every extreme that they name: `far_frames`: for query block r of frame f, entry j - 1 (j = 1 to 6) is a frame f - d and entry 5 + j a frame f + d, with 2**j <= d < 2**(j+1), or -1 where no frame of the video lies at such a distance on that side. In the first query block of each frame every such entry is the farthest frame that the band allows on that side.
All inputs are finite; a program needn't handle non-finite values.
Results may differ from a plain program's by a relative error of at most 0.012.
The roundings to bfloat16 on the way count: a program that leaves them out, or rounds other values in their place, can miss the bound.
Values may be sent and summed in bfloat16 or wider, within the bound.
A program may use at most 128 MiB of HBM per device.

v0:
```python
import jax
import jax.numpy as jnp
from jax import lax
from jax.sharding import PartitionSpec as P

HEAD_DIM = 128
BLOCK = 64
NFAR = 12


epsilon = 1e-06
masked = -1e30


def with_halo(x, sides, width):
    for axis, dim in sides:
        peers, length = (lax.axis_size(axis), x.shape[dim])
        up = [(i, (i + 1) % peers) for i in range(peers - 1)]
        down = [(j, i) for i, j in up]
        last = lax.slice_in_dim(x, length - width, length, axis=dim)
        leading = lax.slice_in_dim(x, 0, width, axis=dim)
        before = lax.ppermute(last, axis, up)
        after = lax.ppermute(leading, axis, down)
        x = jnp.concatenate([before, x, after], axis=dim)
    return x


def heads_lead(blocks):
    return jnp.moveaxis(blocks, 3, 0)


def local(query, key, value, q_gain, k_gain, far_frames, far_pick):
    tok_rows, local_width = query.shape
    full_width = local_width * lax.axis_size("head")
    frame_count = lax.axis_size("tm")
    my_frame = lax.axis_index("tm")
    block_count = tok_rows // BLOCK
    local_heads = local_width // HEAD_DIM
    query_sq = jnp.sum(jnp.square(query.astype(jnp.float32)), axis=1)
    key_sq = jnp.sum(jnp.square(key.astype(jnp.float32)), axis=1)
    query_tot, key_tot = lax.psum((query_sq, key_sq), "head")
    q_norm = (
        query.astype(jnp.float32)
        * lax.rsqrt(query_tot / full_width + epsilon)[:, None]
        * q_gain[None, :]
    ).astype(jnp.bfloat16)
    k_norm = (
        key.astype(jnp.float32)
        * lax.rsqrt(key_tot / full_width + epsilon)[:, None]
        * k_gain[None, :]
    ).astype(jnp.bfloat16)
    stacked = jnp.stack([k_norm, value])
    near_pair = with_halo(stacked, (("tm", 1),), tok_rows)
    wanted = lax.dynamic_slice_in_dim(far_pick, my_frame, 1, 1)[:, 0]
    outgoing = jnp.take(stacked.reshape(2, block_count, BLOCK, local_width), wanted, axis=1)
    incoming = lax.all_to_all(outgoing, "tm", split_axis=1, concat_axis=1, tiled=True)
    far_all = heads_lead(incoming.reshape(2, frame_count, BLOCK, local_heads, HEAD_DIM))
    my_lists = lax.dynamic_slice_in_dim(far_frames, my_frame * block_count, block_count, 0)
    list_ok = my_lists >= 0
    sources = jnp.maximum(my_lists, 0)
    key_frame = my_frame - 1 + jnp.arange(3 * tok_rows) // tok_rows
    near_ok = (key_frame >= 0) & (key_frame < frame_count)
    far_ok = jnp.repeat(list_ok, BLOCK, axis=1)
    score_scale = HEAD_DIM ** (-0.5)

    def one_head(head_index):
        head_start = head_index * HEAD_DIM
        q_head = lax.dynamic_slice_in_dim(q_norm, head_start, HEAD_DIM, 1)
        near_head = lax.dynamic_slice_in_dim(near_pair, head_start, HEAD_DIM, 2)
        far_head = lax.dynamic_index_in_dim(far_all, head_index, 0, keepdims=False)
        far_head = jnp.take(far_head, sources, axis=1).reshape(
            2, block_count, NFAR * BLOCK, HEAD_DIM
        )
        near_score = (
            lax.dot_general(
                q_head, near_head[0], (((1,), (1,)), ((), ())), preferred_element_type=jnp.float32
            )
            * score_scale
        )
        near_score = jnp.where(near_ok[None, :], near_score, masked).reshape(
            block_count, BLOCK, 3 * tok_rows
        )
        far_score = (
            jnp.einsum(
                "nhs,nos->nho",
                q_head.reshape(block_count, BLOCK, HEAD_DIM),
                far_head[0],
                preferred_element_type=jnp.float32,
            )
            * score_scale
        )
        far_score = jnp.where(far_ok[:, None, :], far_score, masked)
        row_peak = jnp.maximum(near_score.max(-1), far_score.max(-1))[..., None]
        near_prob = jnp.exp(near_score - row_peak)
        far_prob = jnp.exp(far_score - row_peak)
        prob_sum = near_prob.sum(-1) + far_prob.sum(-1)
        near_out = jnp.dot(
            near_prob.astype(jnp.bfloat16).reshape(tok_rows, 3 * tok_rows),
            near_head[1],
            preferred_element_type=jnp.float32,
        ).reshape(block_count, BLOCK, HEAD_DIM)
        far_out = jnp.einsum(
            "fkm,fmp->fkp",
            far_prob.astype(jnp.bfloat16),
            far_head[1],
            preferred_element_type=jnp.float32,
        )
        result = ((near_out + far_out) / prob_sum[..., None]).astype(jnp.bfloat16)
        return result.reshape(tok_rows, HEAD_DIM)

    per_head = lax.map(one_head, jnp.arange(local_heads))
    return jnp.transpose(per_head, (1, 0, 2)).reshape(tok_rows, local_width)


def solution(mesh):
    placed = (P("tm", "head"), P("tm", "head"), P("tm", "head"), P("head"), P("head"), P(), P())
    return jax.shard_map(
        local, mesh=mesh, in_specs=placed, out_specs=P("tm", "head"), check_vma=False
    )
```

profile of v0, /device:TPU:201, one launch (start us, length us, event | category | flops | bytes accessed | tf_op | source)
XLA Modules:
  0.0 534.2 jit_solution(15049399553013617098)
XLA Ops:
  0.0 1.0 fusion.30
  1.1 0.9 and_reduce_fusion
  2.0 1.6 fusion.24
  3.6 17.8 %all-reduce = (f32[512]{0:T(512)S(1)}, f32[512]{0:T(512)S(1)}) all-reduce(f32[512]{0:T(512)S(1)} %get-tuple-element.122, f32[512]{0:T(512)S(1)} %get-tuple-element.123), channel_id=1, replica_groups=mesh['tm'=64,'head'=8] {'head'}, use_global_device_ids=true, to_apply=%region_1.0 | all-reduce | flops 1024 | bytes 8192 | tf_op jit(solution)/shard_map/psum | solution.py:41
  21.5 0.9 fusion.29
  22.6 6.6 %gather_fusion.1 = bf16[64,2,64,640]{3,2,1,0:T(8,128)(2,1)} fusion(bf16[2,8,64,640]{3,2,1,0:T(8,128)(2,1)S(1)} %pad_maximum_fusion.2, s32[1024]{0:T(1024)S(1)} %pad_clamp_fusion.1), kind=kCustom, calls=%fused_computation.1 | custom fusion | bytes 20971776 | tf_op jit(solution)/shard_map/jit(_take)/gather | solution.py:55
  29.1 10.1 %select_bitcast_fusion = bf16[2,64,64,640]{3,2,0,1:T(8,128)(2,1)} fusion(bf16[64,2,64,640]{3,2,1,0:T(8,128)(2,1)} %gather_fusion.1, pred[64]{0:T(512)(128)(4,1)S(1)} %and_reduce_fusion), kind=kLoop, calls=%fused_computation.42 | loop fusion | flops 5242880 | bytes 20971584 | tf_op jit(solution)/shard_map/jit(_take)/select_n | solution.py:55
  39.2 10.8 %all-to-all-start = ((bf16[2,64,64,640]{3,2,0,1:T(8,128)(2,1)}), bf16[2,64,64,640]{3,2,0,1:T(8,128)(2,1)}, u32[]{:S(2)}, u32[]{:S(2)}) async-start(bf16[2,64,64,640]{3,2,0,1:T(8,128)(2,1)} %select_bitcast_fusion), calls=%async_computation | async-start | bytes 20971520 | tf_op jit(solution)/shard_map/all_to_all | solution.py:56
  50.3 1.2 pad_maximum_fusion.1
  51.5 3.1 collective-permute-start
  54.6 2.4 collective-permute-start.1
  57.2 1.1 fusion.26
  58.3 290.2 %collective-permute-done = bf16[2,512,640]{2,1,0:T(8,128)(2,1)} collective-permute-done((bf16[2,512,640]{2,1,0:T(8,128)(2,1)}, bf16[2,512,640]{2,1,0:T(8,128)(2,1)}, u32[]{:S(2)}, u32[]{:S(2)}) %collective-permute-start) | collective-permute-done | bytes 1310752 | tf_op jit(solution)/shard_map/ppermute | solution.py:22
  348.5 6.7 %pad_maximum_fusion = bf16[2,1536,640]{2,1,0:T(8,128)(2,1)} fusion(bf16[2,512,640]{2,1,0:T(8,128)(2,1)} %collective-permute-done.1, bf16[1,512,640]{2,1,0:T(8,128)(2,1)S(1)} %bitcast.82, bf16[1,512,640]{2,1,0:T(8,128)(2,1)S(1)} %fusion.38, bf16[2,512,640]{2,1,0:T(8,128)(2,1)} %collective-permute-done), kind=kLoop, calls=%fused_computation.43 | loop fusion | flops 15728640 | bytes 7864320 | tf_op jit(solution)/shard_map/concatenate | solution.py:24
  355.2 9.2 %copy.17 = bf16[2,64,64,640]{3,2,1,0:T(8,128)(2,1)} copy(bf16[2,64,64,640]{3,2,0,1:T(8,128)(2,1)} %all-to-all-done) | data formatting | bytes 20971520 | tf_op jit(solution)/shard_map/all_to_all | solution.py:56
  364.4 23.6 %reshape.78 = bf16[2,64,64,5,128]{4,3,2,1,0:T(8,128)(2,1)} reshape(bf16[2,64,64,640]{3,2,1,0:T(8,128)(2,1)} %copy.17) | data formatting | bytes 20971520 | tf_op jit(solution)/shard_map/reshape | solution.py:57
  388.0 12.4 %copy.18 = bf16[5,2,64,64,128]{4,3,2,1,0:T(8,128)(2,1)} copy(bf16[5,2,64,64,128]{4,0,3,2,1:T(8,128)(2,1)} %bitcast.77) | data formatting | bytes 20971520
  400.3 131.6 %while.11 = (s32[]{:T(128)}, bf16[5,512,128]{1,2,0:T(8,128)(2,1)}, s32[5]{0:T(128)S(1)}, bf16[512,640]{1,0:T(8,128)(2,1)}, bf16[2,1536,640]{2,1,0:T(8,128)(2,1)}...) while((s32[]{:T(128)}, bf16[5,512,128]{1,2,0:T(8,128)(2,1)}, ...), condition=%wide.region_9.10_spmd.clone, body=%wide.region_4.9_spmd.clone.sunk | while | flops 613240192 | bytes 42944168 | solution.py:111
  401.7 0.9 constant_dynamic-slice_fusion.4
  404.7 1.8 dynamic-slice_bitcast_fusion.8
  406.6 2.7 gather_fusion
  409.3 2.2 fusion.60
  411.5 1.8 fusion.61
  413.6 2.2 fusion.62
  415.7 3.3 fusion.59
  419.7 3.5 fusion.63
  423.3 2.0 fusion.64
  428.0 0.9 constant_dynamic-slice_fusion.4
  431.0 1.8 dynamic-slice_bitcast_fusion.8
  432.9 2.7 gather_fusion
  435.6 2.2 fusion.60
  437.9 1.8 fusion.61
  439.9 2.2 fusion.62
  442.1 3.3 fusion.59
  446.0 3.5 fusion.63
  449.6 2.0 fusion.64
  454.4 0.9 constant_dynamic-slice_fusion.4
  457.4 1.8 dynamic-slice_bitcast_fusion.8
  459.2 2.7 gather_fusion
  462.0 2.2 fusion.60
  464.2 1.8 fusion.61
  466.2 2.2 fusion.62
  468.4 3.3 fusion.59
  472.3 3.5 fusion.63
  476.0 2.0 fusion.64
  480.7 0.9 constant_dynamic-slice_fusion.4
  483.7 1.8 dynamic-slice_bitcast_fusion.8
  485.5 2.7 gather_fusion
  488.3 2.2 fusion.60
  490.5 1.8 fusion.61
  492.5 2.2 fusion.62
  494.7 3.3 fusion.59
  498.7 3.5 fusion.63
  502.3 2.0 fusion.64
  507.0 0.9 constant_dynamic-slice_fusion.4
  510.0 1.8 dynamic-slice_bitcast_fusion.8
  511.9 2.7 gather_fusion
  514.6 2.2 fusion.60
  516.8 1.8 fusion.61
  518.9 2.2 fusion.62
  521.0 3.3 fusion.59
  525.0 3.5 fusion.63
  528.6 2.0 fusion.64
  532.0 2.2 copy.20
  (117 shorter events, 15.2 us)
Async XLA Ops:
  0.0 57.0 %copy-start = (s32[512,12]{0,1:T(8,128)S(1)}, s32[512,12]{0,1:T(8,128)}, u32[]{:S(2)}) copy-start(s32[512,12]{0,1:T(8,128)} %param.14) | copy-start | bytes 73732
  0.0 21.5 %copy-start.2 = (bf16[512,640]{1,0:T(8,128)(2,1)S(1)}, bf16[512,640]{1,0:T(8,128)(2,1)}, u32[]{:S(2)}) copy-start(bf16[512,640]{1,0:T(8,128)(2,1)} %param.10) | copy-start | bytes 1966084
  0.0 22.4 %copy-start.3 = (bf16[512,640]{1,0:T(8,128)(2,1)S(1)}, bf16[512,640]{1,0:T(8,128)(2,1)}, u32[]{:S(2)}) copy-start(bf16[512,640]{1,0:T(8,128)(2,1)} %param.11) | copy-start | bytes 1966084
  39.2 10.8 %copy-start.5 = (f32[640]{0:T(1024)S(1)}, f32[640]{0:T(1024)}, u32[]{:S(2)}) copy-start(f32[640]{0:T(1024)} %param.13) | copy-start | bytes 7684
  39.2 316.0 %all-to-all-start = ((bf16[2,64,64,640]{3,2,0,1:T(8,128)(2,1)}), bf16[2,64,64,640]{3,2,0,1:T(8,128)(2,1)}, u32[]{:S(2)}, u32[]{:S(2)}) async-start(bf16[2,64,64,640]{3,2,0,1:T(8,128)(2,1)} %select_bitcast_fusion), calls=%async_computation | async-start | bytes 20971520 | tf_op jit(solution)/shard_map/all_to_all | solution.py:56
  50.3 6.9 %copy-start.4 = (bf16[512,640]{1,0:T(8,128)(2,1)S(1)}, bf16[512,640]{1,0:T(8,128)(2,1)}, u32[]{:S(2)}) copy-start(bf16[512,640]{1,0:T(8,128)(2,1)} %param.9) | copy-start | bytes 1966084
  50.3 6.9 %copy-start.6 = (f32[640]{0:T(1024)S(1)}, f32[640]{0:T(1024)}, u32[]{:S(2)}) copy-start(f32[640]{0:T(1024)} %param.12) | copy-start | bytes 7684
  51.5 297.0 %collective-permute-start = (bf16[2,512,640]{2,1,0:T(8,128)(2,1)}, bf16[2,512,640]{2,1,0:T(8,128)(2,1)}, u32[]{:S(2)}, u32[]{:S(2)}) collective-permute-start(bf16[2,512,640]{2,1,0:T(8,128)(2,1)} %pad_maximum_fusion.1), channel_id=1, source_target_pairs={{0,8},{8,16},{16,24},{24,32},{32,40},{40,48},{48,56},{56,64},{64,7... | collective-permute-start | bytes 3932168 | tf_op jit(solution)/shard_map/ppermute | solution.py:22
  54.6 293.9 %collective-permute-start.1 = (bf16[2,512,640]{2,1,0:T(8,128)(2,1)}, bf16[2,512,640]{2,1,0:T(8,128)(2,1)}, u32[]{:S(2)}, u32[]{:S(2)}) collective-permute-start(bf16[2,512,640]{2,1,0:T(8,128)(2,1)} %pad_maximum_fusion.1), channel_id=1, source_target_pairs={{8,0},{16,8},{24,16},{32,24},{40,32},{48,40},{56,48},{64,56},{72,6... | collective-permute-start | bytes 3932168 | tf_op jit(solution)/shard_map/ppermute | solution.py:23
  532.0 2.2 copy-start.1
where the time goes:
time: 536 us; the launch traced here: 534 us
  waiting for transfers between devices  290 us (54%)
  local copies, waits for them, and re-layouts  99.9 us (19%)
  other arithmetic  55.3 us (10%)
  matrix products  40.2 us (8%)
  blocking collectives  17.8 us (3%)
  starting transfers between devices  16.3 us (3%)
  loops' own time  14.2 us (3%)
    ppermute x1, waiting for transfers between devices, with_halo(): before = lax.ppermute(last, axis, up)  290 us
    reshape x1, local copies, waits for them, and re-layouts, local(): incoming.reshape(2, frame_count, BLOCK, local_heads, HEAD_DIM)  23.6 us
    reduce_sum x10, other arithmetic, one_head(): prob_sum = near_prob.sum(-1) + far_prob.sum(-1)  19.9 us
    psum x1, blocking collectives, local(): query_tot, key_tot = lax.psum((query_sq, key_sq), 'head')  17.8 us
    dot_general x5, matrix products, one_head(): lax.dot_general(q_head, near_head[0], (((1,), (1,)), ((), ())), preferred...  16.7 us
    another operation x1, loops' own time, local(): per_head = lax.map(one_head, jnp.arange(local_heads))  14.2 us
    gather x5, local copies, waits for them, and re-layouts, one_head(): jnp.take(far_head, sources, axis=1)  13.6 us
    unnamed x16, local copies, waits for them, and re-layouts  12.5 us
  transfers between devices with their start and end apart: 3, of which 1 were waited for; matrix products, arithmetic and copies ran while one was open for 2% of the time, Pallas kernels for 0%

commit v1 on v0

v1 whole, which is shorter than its diff:
```python
import functools

import jax
import jax.numpy as jnp
from jax import lax
from jax.experimental import pallas as pl
from jax.experimental.pallas import tpu as pltpu
from jax.sharding import PartitionSpec as P

HEAD_DIM = 128
BLOCK = 64
NFAR = 12
SIDE = 4
HEADS = 5
BLOCKS = 8
FRAMES = 64
GROUPS = 8
TOK = BLOCK * BLOCKS
WIDTH = HEADS * HEAD_DIM
FULL = WIDTH * GROUPS
SLOTS = (0, 1, 2, 3, 4, 6, 7, 8, 9, 10)
FARK = len(SLOTS) * BLOCK
NEARK = 3 * TOK
epsilon = 1e-06
masked = -1e30
MESH = pl.DeviceIdType.MESH
PLANE = (
    (1, 0), (0, 1), (3, 0), (0, 3), (2, 0), (0, 2), (1, 1), (3, 3),
    (1, 3), (3, 1), (2, 1), (1, 2), (2, 3), (3, 2), (2, 2),
)
PEERS = len(PLANE)


def spread_kernel(
    q, k, v, qg, kg, pick, qn_o, near_o, far_o,
    zbuf, out, own, nbuf, sums, parts,
    zs, zr, fs, fr, ns, nr, hs, hr, ls,
):
    frame = lax.axis_index("tm")
    group = lax.axis_index("head")
    col, z = frame // SIDE, frame % SIDE
    x, y = col // SIDE, col % SIDE

    def tm(dev):
        return {"tm": dev}

    def plane_peer(d):
        return (((x + d[0]) % SIDE) * SIDE + (y + d[1]) % SIDE) * SIDE + z

    has_next, has_prev = col < 15, col > 0
    from_prev = jnp.logical_and(z == 0, has_prev)
    from_next = jnp.logical_and(z == SIDE - 1, has_next)
    next_dev = (col + 1) * SIDE
    prev_dev = (col - 1) * SIDE + SIDE - 1

    barrier = pltpu.get_barrier_semaphore()

    def greet(dev):
        pl.semaphore_signal(barrier, inc=1, device_id=dev, device_id_type=MESH)

    for d in PLANE:
        greet(tm(plane_peer(d)))
    for j in range(1, GROUPS):
        greet({"head": (group + j) % GROUPS})

    @pl.when(z > 0)
    def _():
        greet(tm(frame - 1))

    @pl.when(z < SIDE - 1)
    def _():
        greet(tm(frame + 1))

    @pl.when(has_next)
    def _():
        greet(tm(next_dev))

    @pl.when(has_prev)
    def _():
        greet(tm(prev_dev))

    @pl.when(from_prev)
    def _():
        for j in range(SIDE):
            greet(tm((col - 1) * SIDE + j))

    @pl.when(from_next)
    def _():
        for j in range(SIDE):
            greet(tm((col + 1) * SIDE + j))

    for h in range(HEADS):
        zbuf[0, z, h] = v[:, h * HEAD_DIM:(h + 1) * HEAD_DIM].reshape(BLOCKS, BLOCK, HEAD_DIM)
    lane = lax.broadcasted_iota(jnp.int32, (TOK, HEAD_DIM), 1)
    q_part = jnp.sum(jnp.square(q[...].astype(jnp.float32)), axis=1, keepdims=True)
    k_part = jnp.sum(jnp.square(k[...].astype(jnp.float32)), axis=1, keepdims=True)
    both = jnp.where(lane == 0, q_part, jnp.where(lane == 1, k_part, 0.0))
    sums[...] = jnp.transpose(both)[:8]

    lacks_near = jnp.logical_or(frame == 0, frame == FRAMES - 1)

    @pl.when(lacks_near)
    def _():
        nbuf[...] = jnp.zeros_like(nbuf)

    greeted = PEERS + GROUPS - 1
    for cond, n in (
        (z > 0, 1), (z < SIDE - 1, 1), (has_next, 1), (has_prev, 1),
        (from_prev, SIDE), (from_next, SIDE),
    ):
        greeted = greeted + jnp.where(cond, n, 0)
    pl.semaphore_wait(barrier, greeted)

    sum_copies = []
    for j in range(1, GROUPS):
        c = pltpu.make_async_remote_copy(
            sums, parts.at[j], hs.at[j], hr.at[j],
            device_id={"head": (group + j) % GROUPS}, device_id_type=MESH)
        c.start()
        sum_copies.append(c)

    def z_copy(t, j, hop, right):
        dev = frame + 1 if right else frame - 1
        return pltpu.make_async_remote_copy(
            zbuf.at[t, j], zbuf.at[t, j], zs.at[int(right), hop, t], zr.at[j, t],
            device_id=tm(dev), device_id_type=MESH)

    def near_copy(t, up):
        part = pl.ds(2 * z, 2)
        return pltpu.make_async_remote_copy(
            zbuf.at[t, SIDE - 1 if up else 0, :, part], nbuf.at[t, :, part],
            ns.at[int(up), t], nr.at[t],
            device_id=tm(next_dev if up else prev_dev), device_id_type=MESH)

    def step_frame(s):
        if s == 0:
            return z
        if s == SIDE - 1:
            return jnp.where(z < 2, SIDE - 1, 0)
        table = {1: (1, 0, 3, 2), 2: (2, 2, 1, 1)}[s]
        r = jnp.int32(table[0])
        for i in range(1, SIDE):
            r = jnp.where(z == i, table[i], r)
        return r

    def far_copy(s, t, i, j):
        return pltpu.make_async_remote_copy(
            out.at[s, t, i], far_o.at[t, col * SIDE + j], fs.at[s, t], fr.at[s, t],
            device_id=tm(plane_peer(PLANE[i])), device_id_type=MESH)

    def round_(s, t):
        if s == 0:
            @pl.when(z < SIDE - 1)
            def _():
                z_copy(t, z, 0, True).start()

            @pl.when(z > 0)
            def _():
                z_copy(t, z, 0, False).start()
        else:
            @pl.when(z - s >= 0)
            def _():
                z_copy(t, z - s, s, True).wait_recv()

                @pl.when(z < SIDE - 1)
                def _():
                    z_copy(t, z - s, s, True).start()

            @pl.when(z + s < SIDE)
            def _():
                z_copy(t, z + s, s, False).wait_recv()

                @pl.when(z > 0)
                def _():
                    z_copy(t, z + s, s, False).start()

        @pl.when(jnp.logical_and(z == SIDE - 1 - s, has_next))
        def _():
            near_copy(t, True).start()

        @pl.when(jnp.logical_and(z == s, has_prev))
        def _():
            near_copy(t, False).start()

        j = step_frame(s)
        g = col * SIDE + j
        picks = [pick[plane_peer(d), g] for d in PLANE] + [pick[frame, g]]

        def one_head(h, _):
            blocks = [zbuf[t, j, h, b] for b in range(BLOCKS)]
            for i, p in enumerate(picks):
                level = blocks
                for bit in range(3):
                    odd = ((p // (1 << bit)) % 2) == 1
                    level = [jnp.where(odd, level[2 * m + 1], level[2 * m]) for m in range(len(level) // 2)]
                if i < PEERS:
                    out[s, t, i, h] = level[0]
                else:
                    own[t, j, h] = level[0]
            return _

        lax.fori_loop(0, HEADS, one_head, 0)
        for i in range(PEERS):
            far_copy(s, t, i, j).start()
        pltpu.make_async_copy(own.at[t, j], far_o.at[t, g], ls.at[0, s, t]).start()

    round_(0, 0)
    for c in sum_copies:
        c.wait()
    total = sums[...]
    for j in range(1, GROUPS):
        total = total + parts[j]
    total = jnp.concatenate([total, jnp.zeros((HEAD_DIM - 8, TOK), jnp.float32)], axis=0)
    scale = lax.rsqrt(jnp.transpose(total) / FULL + epsilon)
    q_scale, k_scale = scale[:, 0:1], scale[:, 1:2]
    for h in range(HEADS):
        cut = slice(h * HEAD_DIM, (h + 1) * HEAD_DIM)
        k_norm = (k[:, cut].astype(jnp.float32) * k_scale * kg[:, cut]).astype(jnp.bfloat16)
        zbuf[1, z, h] = k_norm.reshape(BLOCKS, BLOCK, HEAD_DIM)
        qn_o[h] = (q[:, cut].astype(jnp.float32) * q_scale * qg[:, cut]).astype(jnp.bfloat16)
    round_(0, 1)
    for s in range(1, SIDE):
        for t in range(2):
            round_(s, t)

    @pl.when(jnp.logical_or(from_prev, from_next))
    def _():
        for t in range(2):
            pltpu.make_async_copy(nbuf.at[t], nbuf.at[t], nr.at[t]).wait()

    def near_out(t, place, src):
        return pltpu.make_async_copy(src, near_o.at[t, place], ls.at[1, place, t])

    for t in range(2):
        near_out(t, 1, zbuf.at[t, z]).start()

        @pl.when(z > 0)
        def _():
            near_out(t, 0, zbuf.at[t, z - 1]).start()

        @pl.when(z == 0)
        def _():
            near_out(t, 0, nbuf.at[t]).start()

        @pl.when(z < SIDE - 1)
        def _():
            near_out(t, 2, zbuf.at[t, z + 1]).start()

        @pl.when(z == SIDE - 1)
        def _():
            near_out(t, 2, nbuf.at[t]).start()

    for t in range(2):
        for place in range(3):
            near_out(t, place, nbuf.at[t]).wait()
        for s in range(SIDE):
            pltpu.make_async_copy(own.at[t, 0], far_o.at[t, 0], ls.at[0, s, t]).wait()
            pltpu.make_async_copy(out.at[s, t], out.at[s, t], fs.at[s, t]).wait()
            pltpu.make_async_copy(out.at[s, t], out.at[s, t], fr.at[s, t]).wait()

            @pl.when(jnp.logical_and(z - s >= 0, z < SIDE - 1))
            def _():
                z_copy(t, z - s, s, True).wait_send()

            @pl.when(jnp.logical_and(z + s < SIDE, z > 0))
            def _():
                z_copy(t, z + s, s, False).wait_send()

        @pl.when(has_next)
        def _():
            near_copy(t, True).wait_send()

        @pl.when(has_prev)
        def _():
            near_copy(t, False).wait_send()


def spread(query, key, value, q_gain, k_gain, far_pick):
    vmem = pl.BlockSpec(memory_space=pltpu.VMEM)
    hbm = pl.BlockSpec(memory_space=pl.ANY)
    dma = pltpu.SemaphoreType.DMA
    bf = jnp.bfloat16
    return pl.pallas_call(
        spread_kernel,
        out_shape=(
            jax.ShapeDtypeStruct((HEADS, TOK, HEAD_DIM), bf),
            jax.ShapeDtypeStruct((2, 3, HEADS, BLOCKS, BLOCK, HEAD_DIM), bf),
            jax.ShapeDtypeStruct((2, FRAMES, HEADS, BLOCK, HEAD_DIM), bf),
        ),
        in_specs=[vmem] * 5 + [pl.BlockSpec(memory_space=pltpu.SMEM)],
        out_specs=(vmem, hbm, hbm),
        scratch_shapes=[
            pltpu.VMEM((2, SIDE, HEADS, BLOCKS, BLOCK, HEAD_DIM), bf),
            pltpu.VMEM((SIDE, 2, PEERS, HEADS, BLOCK, HEAD_DIM), bf),
            pltpu.VMEM((2, SIDE, HEADS, BLOCK, HEAD_DIM), bf),
            pltpu.VMEM((2, HEADS, BLOCKS, BLOCK, HEAD_DIM), bf),
            pltpu.VMEM((8, TOK), jnp.float32),
            pltpu.VMEM((GROUPS, 8, TOK), jnp.float32),
            dma((2, SIDE, 2)), dma((SIDE, 2)),
            dma((SIDE, 2)), dma((SIDE, 2)),
            dma((2, 2)), dma((2,)),
            dma((GROUPS,)), dma((GROUPS,)),
            dma((2, SIDE, 2)),
        ],
        compiler_params=pltpu.CompilerParams(
            collective_id=0, has_side_effects=True, vmem_limit_bytes=48 << 20),
    )(query, key, value, q_gain, k_gain, far_pick)


def attend_kernel(lists, q, near, far, o):
    tile = pl.program_id(1)
    rows = q.shape[1]
    per_tile = rows // BLOCK
    frame = lists[NFAR * BLOCKS]
    rate = HEAD_DIM ** (-0.5) * 1.4426950408889634
    keys = near[1, :, 0].reshape(NEARK, HEAD_DIM)
    vals = near[0, :, 0].reshape(NEARK, HEAD_DIM)
    dims = (((1,), (1,)), ((), ()))
    place = lax.broadcasted_iota(jnp.int32, (1, NEARK), 1) // TOK
    near_ok = jnp.logical_and(
        jnp.logical_or(place > 0, frame > 0), jnp.logical_or(place < 2, frame < FRAMES - 1))
    near_s = lax.dot_general(q[0], keys, dims, preferred_element_type=jnp.float32)
    near_s = jnp.where(near_ok, near_s, masked)
    slot = lax.broadcasted_iota(jnp.int32, (1, FARK), 1) // BLOCK
    far_s, picked = [], []
    for b in range(per_tile):
        sources = [lists[(tile * per_tile + b) * NFAR + s] for s in SLOTS]
        bias = jnp.zeros((1, FARK), jnp.float32)
        for i, g in enumerate(sources):
            bias = jnp.where(slot == i, jnp.where(g >= 0, 0.0, masked), bias)
        held = [jnp.maximum(g, 0) for g in sources]
        far_k = jnp.concatenate([far[1, g, 0] for g in held], axis=0)
        picked.append(held)
        far_s.append(lax.dot_general(
            q[0, b * BLOCK:(b + 1) * BLOCK], far_k, dims, preferred_element_type=jnp.float32) + bias)
    far_s = jnp.concatenate(far_s, axis=0)
    peak = jnp.maximum(near_s.max(-1, keepdims=True), far_s.max(-1, keepdims=True))
    near_p = jnp.exp2((near_s - peak) * rate)
    far_p = jnp.exp2((far_s - peak) * rate)
    total = near_p.sum(-1, keepdims=True) + far_p.sum(-1, keepdims=True)
    near_o = jnp.dot(near_p.astype(jnp.bfloat16), vals, preferred_element_type=jnp.float32)
    far_p = far_p.astype(jnp.bfloat16)
    far_o = []
    for b in range(per_tile):
        far_v = jnp.concatenate([far[0, g, 0] for g in picked[b]], axis=0)
        far_o.append(jnp.dot(
            far_p[b * BLOCK:(b + 1) * BLOCK], far_v, preferred_element_type=jnp.float32))
    o[...] = ((near_o + jnp.concatenate(far_o, axis=0)) / total).astype(jnp.bfloat16)


def attend(lists, q, near, far, rows=256):
    near = near.reshape(2, 3, HEADS, TOK, HEAD_DIM)
    return pl.pallas_call(
        attend_kernel,
        out_shape=jax.ShapeDtypeStruct((TOK, WIDTH), jnp.bfloat16),
        grid_spec=pltpu.PrefetchScalarGridSpec(
            num_scalar_prefetch=1,
            grid=(HEADS, TOK // rows),
            in_specs=[
                pl.BlockSpec((1, rows, HEAD_DIM), lambda h, i, _: (h, i, 0)),
                pl.BlockSpec((2, 3, 1, TOK, HEAD_DIM), lambda h, i, _: (0, 0, h, 0, 0)),
                pl.BlockSpec((2, FRAMES, 1, BLOCK, HEAD_DIM), lambda h, i, _: (0, 0, h, 0, 0)),
            ],
            out_specs=pl.BlockSpec((rows, HEAD_DIM), lambda h, i, _: (i, h)),
        ),
        compiler_params=pltpu.CompilerParams(vmem_limit_bytes=48 << 20),
    )(lists, q, near, far)


def local(query, key, value, q_gain, k_gain, far_frames, far_pick):
    frame = lax.axis_index("tm")
    mine = lax.dynamic_slice_in_dim(far_frames, frame * BLOCKS, BLOCKS, 0)
    lists = jnp.concatenate([mine.reshape(-1), frame.reshape(1).astype(jnp.int32)])
    q_norm, near, far = spread(
        query, key, value, q_gain.reshape(1, WIDTH), k_gain.reshape(1, WIDTH), far_pick)
    return attend(lists, q_norm, near, far)


def solution(mesh):
    placed = (P("tm", "head"), P("tm", "head"), P("tm", "head"), P("head"), P("head"), P(), P())
    return jax.shard_map(
        local, mesh=mesh, in_specs=placed, out_specs=P("tm", "head"), check_vma=False
    )
```

time: 536 us -> 201 us (0.38)
  the two profiles are of different devices: /device:TPU:201 before, /device:TPU:8 now
where the time goes in v1:
time: 201 us; the launch traced here: 200 us
  Pallas kernels  192 us (96%)
  local copies, waits for them, and re-layouts  7.75 us (4%)
    pallas_call x1, Pallas kernels, spread(): pl.pallas_call(spread_kernel, out_shape=(jax.ShapeDtypeStruct((HEADS, TOK...  175 us
    pallas_call x1, Pallas kernels, attend(): pl.pallas_call(attend_kernel, out_shape=jax.ShapeDtypeStruct((TOK, WIDTH)...  17.1 us
    unnamed x12, local copies, waits for them, and re-layouts  6.13 us

profile of v1, /device:TPU:8, one launch (start us, length us, event | category | flops | bytes accessed | tf_op | source)
XLA Modules:
  0.0 200.2 jit_solution(16035191292934124208)
XLA Ops:
  0.0 0.0 copy-start
  0.0 0.7 reshape.17.qg
  0.7 0.7 reshape.18.kg
  1.4 0.0 copy-done
  1.4 0.1 constant_dynamic-slice_fusion
  1.5 0.1 copy.8
  1.5 0.1 reshape.15
  1.6 0.1 pad_add_fusion.lists
  1.7 0.0 copy-start.2
  1.7 1.1 copy-done.2
  2.8 0.0 copy-start.3
  2.8 1.1 copy-done.3
  3.9 0.0 copy-start.4
  3.9 1.1 copy-done.4
  5.0 0.0 copy-start.5
  5.0 0.8 copy-done.5
  5.7 175.2 %shard_map.73 = (bf16[5,512,128]{2,1,0:T(8,128)(2,1)S(1)}, bf16[2,3,5,8,64,128]{5,4,3,2,1,0:T(8,128)(2,1)}, bf16[2,64,5,64,128]{4,3,2,1,0:T(8,128)(2,1)}) custom-call(bf16[512,640]{1,0:T(8,128)(2,1)S(1)} %copy-done.2, bf16[512,640]{1,0:T(8,128)(2,1)S(1)} %copy-done.3, bf16[512,640]{1,0:T(8,128)(2,1)S(1)} %copy-done.4, f32[1,640]{1,0:T(1,128)S(1)} %reshape.17.qg, ...), custom_call_target="tpu_custom_call" | custom-call | tf_op jit(solution)/shard_map/pallas_call | solution.py:283
  180.9 0.0 copy-start.1
  180.9 2.1 %copy-done.1 = bf16[2,3,5,8,64,128]{5,4,3,2,1,0:T(8,128)(2,1)S(1)} copy-done((bf16[2,3,5,8,64,128]{5,4,3,2,1,0:T(8,128)(2,1)S(1)}, bf16[2,3,5,8,64,128]{5,4,3,2,1,0:T(8,128)(2,1)}, u32[]{:S(2)}) %copy-start.1) | copy-done | bytes 3932184
  183.0 17.1 %shard_map.74 = bf16[512,640]{1,0:T(8,128)(2,1)} custom-call(s32[97]{0:T(128)S(1)} %pad_add_fusion.lists, bf16[5,512,128]{2,1,0:T(8,128)(2,1)S(1)} %get-tuple-element.8.q, bf16[2,3,5,512,128]{4,3,2,1,0:T(8,128)(2,1)S(1)} %bitcast.2, bf16[2,64,5,64,128]{4,3,2,1,0:T(8,128)(2,1)} %get-tuple-element.10.far), custom_call_target="tpu_custom_call" | custom-call | tf_op jit(solution)/shard_map/pallas_call | solution.py:353
Async XLA Ops:
  0.0 1.4 copy-start
  1.7 1.1 copy-start.2
  2.8 1.1 copy-start.3
  3.9 1.1 copy-start.4
  5.0 0.8 copy-start.5
  180.9 2.1 %copy-start.1 = (bf16[2,3,5,8,64,128]{5,4,3,2,1,0:T(8,128)(2,1)S(1)}, bf16[2,3,5,8,64,128]{5,4,3,2,1,0:T(8,128)(2,1)}, u32[]{:S(2)}) copy-start(bf16[2,3,5,8,64,128]{5,4,3,2,1,0:T(8,128)(2,1)} %get-tuple-element.9) | copy-start | bytes 11796484

commit v2 on v1

v2 whole, which is shorter than its diff:
```python
import functools

import jax
import jax.numpy as jnp
from jax import lax
from jax.experimental import pallas as pl
from jax.experimental.pallas import tpu as pltpu
from jax.sharding import PartitionSpec as P

HEAD_DIM = 128
BLOCK = 64
NFAR = 12
SIDE = 4
HEADS = 5
BLOCKS = 8
FRAMES = 64
GROUPS = 8
TOK = BLOCK * BLOCKS
WIDTH = HEADS * HEAD_DIM
FULL = WIDTH * GROUPS
SLOTS = (0, 1, 2, 3, 4, 6, 7, 8, 9, 10)
FARK = len(SLOTS) * BLOCK
NEARK = 3 * TOK
epsilon = 1e-06
masked = -1e30
MESH = pl.DeviceIdType.MESH
PLANE = (
    (1, 0), (0, 1), (3, 0), (0, 3), (2, 0), (0, 2), (1, 1), (3, 3),
    (1, 3), (3, 1), (2, 1), (1, 2), (2, 3), (3, 2), (2, 2),
)
PEERS = len(PLANE)
HALF = 8
ROWS = 256
RATE = HEAD_DIM ** (-0.5) * 1.4426950408889634
DIMS = (((1,), (1,)), ((), ()))


def spread_kernel(
    q, k, v, qg, kg, pick, qn_o, acc_o, stat_o, far_o,
    q_in, k_in, qn, acc, stat, zbuf, out, own, nbuf, sums, parts,
    ins, zs, zr, fs, fr, ns, nr, hs, hr, ls, os,
):
    frame = lax.axis_index("tm")
    group = lax.axis_index("head")
    col, z = frame // SIDE, frame % SIDE
    x, y = col // SIDE, col % SIDE

    def tm(dev):
        return {"tm": dev}

    def plane_peer(d):
        return (((x + d[0]) % SIDE) * SIDE + (y + d[1]) % SIDE) * SIDE + z

    def cut(h):
        return slice(h * HEAD_DIM, (h + 1) * HEAD_DIM)

    has_next, has_prev = col < 15, col > 0
    from_prev = jnp.logical_and(z == 0, has_prev)
    from_next = jnp.logical_and(z == SIDE - 1, has_next)
    next_dev = (col + 1) * SIDE
    prev_dev = (col - 1) * SIDE + SIDE - 1

    loads = [pltpu.make_async_copy(q, q_in, ins.at[0]), pltpu.make_async_copy(k, k_in, ins.at[1])]
    loads += [pltpu.make_async_copy(v.at[:, cut(h)], zbuf.at[0, z, h], ins.at[2 + h]) for h in range(HEADS)]
    for c in loads:
        c.start()

    barrier = pltpu.get_barrier_semaphore()

    def greet(dev):
        pl.semaphore_signal(barrier, inc=1, device_id=dev, device_id_type=MESH)

    for d in PLANE:
        greet(tm(plane_peer(d)))
    for j in range(1, GROUPS):
        greet({"head": (group + j) % GROUPS})

    @pl.when(z > 0)
    def _():
        greet(tm(frame - 1))

    @pl.when(z < SIDE - 1)
    def _():
        greet(tm(frame + 1))

    @pl.when(has_next)
    def _():
        greet(tm(next_dev))

    @pl.when(has_prev)
    def _():
        greet(tm(prev_dev))

    @pl.when(from_prev)
    def _():
        for j in range(SIDE):
            greet(tm((col - 1) * SIDE + j))

    @pl.when(from_next)
    def _():
        for j in range(SIDE):
            greet(tm((col + 1) * SIDE + j))

    loads[0].wait()
    loads[1].wait()
    lane = lax.broadcasted_iota(jnp.int32, (TOK, HEAD_DIM), 1)
    q_part = jnp.sum(jnp.square(q_in[...].astype(jnp.float32)), axis=1, keepdims=True)
    k_part = jnp.sum(jnp.square(k_in[...].astype(jnp.float32)), axis=1, keepdims=True)
    both = jnp.where(lane == 0, q_part, jnp.where(lane == 1, k_part, 0.0))
    sums[...] = jnp.transpose(both)[:8]

    lacks_near = jnp.logical_or(frame == 0, frame == FRAMES - 1)

    @pl.when(lacks_near)
    def _():
        nbuf[...] = jnp.zeros_like(nbuf)

    for c in loads[2:]:
        c.wait()
    greeted = PEERS + GROUPS - 1
    for cond, n in (
        (z > 0, 1), (z < SIDE - 1, 1), (has_next, 1), (has_prev, 1),
        (from_prev, SIDE), (from_next, SIDE),
    ):
        greeted = greeted + jnp.where(cond, n, 0)
    pl.semaphore_wait(barrier, greeted)

    sum_copies = []
    for j in range(1, GROUPS):
        c = pltpu.make_async_remote_copy(
            sums, parts.at[j], hs.at[j], hr.at[j],
            device_id={"head": (group + j) % GROUPS}, device_id_type=MESH)
        c.start()
        sum_copies.append(c)

    def z_copy(t, j, hop, right):
        dev = frame + 1 if right else frame - 1
        return pltpu.make_async_remote_copy(
            zbuf.at[t, j], zbuf.at[t, j], zs.at[int(right), hop, t], zr.at[j, t],
            device_id=tm(dev), device_id_type=MESH)

    def near_copy(t, up):
        part = pl.ds(2 * BLOCK * z, 2 * BLOCK)
        return pltpu.make_async_remote_copy(
            zbuf.at[t, SIDE - 1 if up else 0, :, part], nbuf.at[t, :, part],
            ns.at[int(up), t], nr.at[t],
            device_id=tm(next_dev if up else prev_dev), device_id_type=MESH)

    def step_frame(s):
        if s == 0:
            return z
        if s == SIDE - 1:
            return jnp.where(z < 2, SIDE - 1, 0)
        table = {1: (1, 0, 3, 2), 2: (2, 2, 1, 1)}[s]
        r = jnp.int32(table[0])
        for i in range(1, SIDE):
            r = jnp.where(z == i, table[i], r)
        return r

    def far_copy(s, t, i, j):
        return pltpu.make_async_remote_copy(
            out.at[s, t, i], far_o.at[t, col * SIDE + j], fs.at[s, t, i // HALF], fr.at[s, t],
            device_id=tm(plane_peer(PLANE[i])), device_id_type=MESH)

    def sent(s, t, half):
        part = out.at[s, t, pl.ds(half * HALF, HALF if half == 0 else PEERS - HALF)]
        return pltpu.make_async_copy(part, part, fs.at[s, t, half])

    def column(s, t):
        if s == 0:
            @pl.when(z < SIDE - 1)
            def _():
                z_copy(t, z, 0, True).start()

            @pl.when(z > 0)
            def _():
                z_copy(t, z, 0, False).start()
        else:
            @pl.when(z - s >= 0)
            def _():
                z_copy(t, z - s, s, True).wait_recv()

                @pl.when(z < SIDE - 1)
                def _():
                    z_copy(t, z - s, s, True).start()

            @pl.when(z + s < SIDE)
            def _():
                z_copy(t, z + s, s, False).wait_recv()

                @pl.when(z > 0)
                def _():
                    z_copy(t, z + s, s, False).start()

        @pl.when(jnp.logical_and(z == SIDE - 1 - s, has_next))
        def _():
            near_copy(t, True).start()

        @pl.when(jnp.logical_and(z == s, has_prev))
        def _():
            near_copy(t, False).start()

    def choose(s, t):
        j = step_frame(s)
        g = col * SIDE + j
        picks = [pick[plane_peer(d), g] for d in PLANE] + [pick[frame, g]]

        def one_head(h, carry):
            blocks = [zbuf[t, j, h, b * BLOCK:(b + 1) * BLOCK] for b in range(BLOCKS)]
            for i, p in enumerate(picks):
                level = blocks
                for bit in range(3):
                    odd = ((p // (1 << bit)) % 2) == 1
                    level = [jnp.where(odd, level[2 * m + 1], level[2 * m]) for m in range(len(level) // 2)]
                if i < PEERS:
                    out[s, t, i, h] = level[0]
                else:
                    own[t, j, h] = level[0]
            return carry

        lax.fori_loop(0, HEADS, one_head, 0)
        pltpu.make_async_copy(own.at[t, j], far_o.at[t, g], ls.at[s, t]).start()

    def post(s, t, half):
        j = step_frame(s)
        for i in range(PEERS):
            if i // HALF == half:
                far_copy(s, t, i, j).start()

    column(0, 0)
    choose(0, 0)
    post(0, 0, 0)
    post(0, 0, 1)
    for c in sum_copies:
        c.wait()
    total = sums[...]
    for j in range(1, GROUPS):
        total = total + parts[j]
    total = jnp.concatenate([total, jnp.zeros((HEAD_DIM - 8, TOK), jnp.float32)], axis=0)
    scale = lax.rsqrt(jnp.transpose(total) / FULL + epsilon)
    q_scale, k_scale = scale[:, 0:1], scale[:, 1:2]
    for h in range(HEADS):
        k_norm = k_in[:, cut(h)].astype(jnp.float32) * k_scale * kg[:, cut(h)]
        zbuf[1, z, h] = k_norm.astype(jnp.bfloat16)
    column(0, 1)
    for h in range(HEADS):
        qn[h] = (q_in[:, cut(h)].astype(jnp.float32) * q_scale * qg[:, cut(h)]).astype(jnp.bfloat16)
    q_out = pltpu.make_async_copy(qn, qn_o, os.at[0])
    q_out.start()
    order = [(s, t) for s in range(SIDE) for t in range(2)]
    for r in range(1, len(order)):
        s, t = order[r]
        choose(s, t)
        sent(*order[r - 1], 0).wait()
        post(s, t, 0)
        if r + 1 < len(order):
            column(*order[r + 1])
        sent(*order[r - 1], 1).wait()
        post(s, t, 1)

    @pl.when(jnp.logical_or(from_prev, from_next))
    def _():
        for t in range(2):
            pltpu.make_async_copy(nbuf.at[t], nbuf.at[t], nr.at[t]).wait()

    def near_rows(t, h):
        prev = jnp.where(z > 0, zbuf[t, jnp.maximum(z - 1, 0), h], nbuf[t, h])
        after = jnp.where(z < SIDE - 1, zbuf[t, jnp.minimum(z + 1, SIDE - 1), h], nbuf[t, h])
        return jnp.concatenate([prev, zbuf[t, z, h], after], axis=0)

    place = lax.broadcasted_iota(jnp.int32, (1, NEARK), 1) // TOK
    near_ok = jnp.logical_and(
        jnp.logical_or(place > 0, frame > 0), jnp.logical_or(place < 2, frame < FRAMES - 1))
    half_lane = lax.broadcasted_iota(jnp.int32, (ROWS, HEAD_DIM), 1) < BLOCK

    def near_tile(n, carry):
        h, i = n // (TOK // ROWS), n % (TOK // ROWS)
        rows = pl.ds(i * ROWS, ROWS)
        score = lax.dot_general(qn[h, rows], near_rows(1, h), DIMS, preferred_element_type=jnp.float32)
        score = jnp.where(near_ok, score, masked)
        peak = score.max(-1, keepdims=True)
        prob = jnp.exp2((score - peak) * RATE)
        total = prob.sum(-1, keepdims=True)
        acc[h, rows] = jnp.dot(
            prob.astype(jnp.bfloat16), near_rows(0, h), preferred_element_type=jnp.float32)
        stat[h, rows] = jnp.where(half_lane, peak, total)
        return carry

    lax.fori_loop(0, HEADS * (TOK // ROWS), near_tile, 0)
    near_out = [pltpu.make_async_copy(acc, acc_o, os.at[1]), pltpu.make_async_copy(stat, stat_o, os.at[2])]
    for c in near_out:
        c.start()

    for t in range(2):
        for s in range(SIDE):
            pltpu.make_async_copy(own.at[t, 0], far_o.at[t, 0], ls.at[s, t]).wait()
            pltpu.make_async_copy(out.at[s, t], out.at[s, t], fr.at[s, t]).wait()

            @pl.when(jnp.logical_and(z - s >= 0, z < SIDE - 1))
            def _():
                z_copy(t, z - s, s, True).wait_send()

            @pl.when(jnp.logical_and(z + s < SIDE, z > 0))
            def _():
                z_copy(t, z + s, s, False).wait_send()

        @pl.when(has_next)
        def _():
            near_copy(t, True).wait_send()

        @pl.when(has_prev)
        def _():
            near_copy(t, False).wait_send()
    sent(*order[-1], 0).wait()
    sent(*order[-1], 1).wait()
    q_out.wait()
    for c in near_out:
        c.wait()


def spread(query, key, value, q_gain, k_gain, far_pick):
    vmem = pl.BlockSpec(memory_space=pltpu.VMEM)
    hbm = pl.BlockSpec(memory_space=pl.ANY)
    dma = pltpu.SemaphoreType.DMA
    bf, f32 = jnp.bfloat16, jnp.float32
    heads = (HEADS, TOK, HEAD_DIM)
    return pl.pallas_call(
        spread_kernel,
        out_shape=(
            jax.ShapeDtypeStruct(heads, bf),
            jax.ShapeDtypeStruct(heads, f32),
            jax.ShapeDtypeStruct(heads, f32),
            jax.ShapeDtypeStruct((2, FRAMES, HEADS, BLOCK, HEAD_DIM), bf),
        ),
        in_specs=[hbm] * 3 + [vmem] * 2 + [pl.BlockSpec(memory_space=pltpu.SMEM)],
        out_specs=(hbm,) * 4,
        scratch_shapes=[
            pltpu.VMEM((TOK, WIDTH), bf),
            pltpu.VMEM((TOK, WIDTH), bf),
            pltpu.VMEM(heads, bf),
            pltpu.VMEM(heads, f32),
            pltpu.VMEM(heads, f32),
            pltpu.VMEM((2, SIDE) + heads, bf),
            pltpu.VMEM((SIDE, 2, PEERS, HEADS, BLOCK, HEAD_DIM), bf),
            pltpu.VMEM((2, SIDE, HEADS, BLOCK, HEAD_DIM), bf),
            pltpu.VMEM((2,) + heads, bf),
            pltpu.VMEM((8, TOK), f32),
            pltpu.VMEM((GROUPS, 8, TOK), f32),
            dma((2 + HEADS,)),
            dma((2, SIDE, 2)), dma((SIDE, 2)),
            dma((SIDE, 2, 2)), dma((SIDE, 2)),
            dma((2, 2)), dma((2,)),
            dma((GROUPS,)), dma((GROUPS,)),
            dma((SIDE, 2)), dma((3,)),
        ],
        compiler_params=pltpu.CompilerParams(
            collective_id=0, has_side_effects=True, vmem_limit_bytes=48 << 20),
    )(query, key, value, q_gain, k_gain, far_pick)


def attend_kernel(lists, q, acc, stat, far, o):
    slot = lax.broadcasted_iota(jnp.int32, (1, FARK), 1) // BLOCK
    scores, picked = [], []
    for b in range(BLOCKS):
        sources = [lists[b * NFAR + s] for s in SLOTS]
        bias = jnp.zeros((1, FARK), jnp.float32)
        for i, g in enumerate(sources):
            bias = jnp.where(slot == i, jnp.where(g >= 0, 0.0, masked), bias)
        held = [jnp.maximum(g, 0) for g in sources]
        far_k = jnp.concatenate([far[1, g, 0] for g in held], axis=0)
        picked.append(held)
        scores.append(lax.dot_general(
            q[0, b * BLOCK:(b + 1) * BLOCK], far_k, DIMS, preferred_element_type=jnp.float32) + bias)
    for b in range(BLOCKS):
        rows = slice(b * BLOCK, (b + 1) * BLOCK)
        near_peak, near_total = stat[0, rows, 0:1], stat[0, rows, BLOCK:BLOCK + 1]
        peak = jnp.maximum(near_peak, scores[b].max(-1, keepdims=True))
        prob = jnp.exp2((scores[b] - peak) * RATE)
        shrink = jnp.exp2((near_peak - peak) * RATE)
        total = near_total * shrink + prob.sum(-1, keepdims=True)
        far_v = jnp.concatenate([far[0, g, 0] for g in picked[b]], axis=0)
        sums = acc[0, rows] * shrink + jnp.dot(
            prob.astype(jnp.bfloat16), far_v, preferred_element_type=jnp.float32)
        o[rows] = (sums / total).astype(jnp.bfloat16)


def attend(lists, q, acc, stat, far):
    head = pl.BlockSpec((1, TOK, HEAD_DIM), lambda h, _: (h, 0, 0))
    return pl.pallas_call(
        attend_kernel,
        out_shape=jax.ShapeDtypeStruct((TOK, WIDTH), jnp.bfloat16),
        grid_spec=pltpu.PrefetchScalarGridSpec(
            num_scalar_prefetch=1,
            grid=(HEADS,),
            in_specs=[head] * 3 + [
                pl.BlockSpec((2, FRAMES, 1, BLOCK, HEAD_DIM), lambda h, _: (0, 0, h, 0, 0)),
            ],
            out_specs=pl.BlockSpec((TOK, HEAD_DIM), lambda h, _: (0, h)),
        ),
        compiler_params=pltpu.CompilerParams(vmem_limit_bytes=48 << 20),
    )(lists, q, acc, stat, far)


def local(query, key, value, q_gain, k_gain, far_frames, far_pick):
    frame = lax.axis_index("tm")
    mine = lax.dynamic_slice_in_dim(far_frames, frame * BLOCKS, BLOCKS, 0)
    held = spread(
        query, key, value, q_gain.reshape(1, WIDTH), k_gain.reshape(1, WIDTH), far_pick)
    return attend(mine.reshape(-1), *held)


def solution(mesh):
    placed = (P("tm", "head"), P("tm", "head"), P("tm", "head"), P("head"), P("head"), P(), P())
    return jax.shard_map(
        local, mesh=mesh, in_specs=placed, out_specs=P("tm", "head"), check_vma=False
    )
```

time: 201 us -> 202 us (level)
  the two profiles are of different devices: /device:TPU:8 before, /device:TPU:252 now
where the time goes in v2:
time: 202 us
  Pallas kernels  196 us (97%)
  local copies, waits for them, and re-layouts  5.65 us (3%)
    pallas_call x1, Pallas kernels, spread(): pl.pallas_call(spread_kernel, out_shape=(jax.ShapeDtypeStruct(heads, bf),...  186 us
    pallas_call x1, Pallas kernels, attend(): pl.pallas_call(attend_kernel, out_shape=jax.ShapeDtypeStruct((TOK, WIDTH)...  10.5 us

profile of v2, /device:TPU:252, one launch (start us, length us, event | category | flops | bytes accessed | tf_op | source)
XLA Modules:
  0.0 201.7 jit_solution(6815920210505233943)
XLA Ops:
  0.0 0.0 copy-start
  0.0 0.7 reshape.10.qg
  0.7 0.7 reshape.11.kg
  1.4 0.0 copy-done
  1.4 0.1 constant_dynamic-slice_fusion
  1.5 0.1 copy.8
  1.5 0.1 reshape.9.lists
  1.6 0.0 copy-start.1
  1.6 1.1 copy-done.1
  2.7 0.0 copy-start.2
  2.7 1.1 copy-done.2
  3.8 0.0 copy-start.3
  3.8 1.1 copy-done.3
  4.9 0.0 copy-start.4
  4.9 0.8 copy-done.4
  5.7 185.5 %shard_map.73 = (bf16[5,512,128]{2,1,0:T(8,128)(2,1)S(1)}, f32[5,512,128]{2,1,0:T(8,128)S(1)}, f32[5,512,128]{2,1,0:T(8,128)S(1)}, bf16[2,64,5,64,128]{4,3,2,1,0:T(8,128)(2,1)}) custom-call(bf16[512,640]{1,0:T(8,128)(2,1)S(1)} %copy-done.1, bf16[512,640]{1,0:T(8,128)(2,1)S(1)} %copy-done.2, bf16[512,640]{1,0:T(8,128)(2,1)S(1)} %copy-done.3, ...), custom_call_target="tpu_custom_call" | custom-call | tf_op jit(solution)/shard_map/pallas_call | solution.py:327
  191.2 10.5 %shard_map.74 = bf16[512,640]{1,0:T(8,128)(2,1)} custom-call(s32[96]{0:T(128)S(1)} %reshape.9.lists, bf16[5,512,128]{2,1,0:T(8,128)(2,1)S(1)} %get-tuple-element.9.q, f32[5,512,128]{2,1,0:T(8,128)S(1)} %get-tuple-element.10.acc, f32[5,512,128]{2,1,0:T(8,128)S(1)} %get-tuple-element.11.stat, bf16[2,64,5,64,128]{4,3,2,1,0:T(8,128)(2,1)} %get-tuple-element.12.far), custom_call_target="tpu_custom_call" | custom-call | tf_op jit(solution)/shard_map/pallas_call | solution.py:389
Async XLA Ops:
  0.0 1.4 copy-start
  1.6 1.1 copy-start.1
  2.7 1.1 copy-start.2
  3.8 1.1 copy-start.3
  4.9 0.8 copy-start.4

commit v3 on v2

--- a/solution.py
+++ b/solution.py
@@ -37,8 +37,8 @@
 
 def spread_kernel(
     q, k, v, qg, kg, pick, qn_o, acc_o, stat_o, far_o,
-    q_in, k_in, qn, acc, stat, zbuf, out, own, nbuf, sums, parts,
-    ins, zs, zr, fs, fr, ns, nr, hs, hr, ls, os,
+    q_in, k_in, qn, acc, stat, zbuf, out, own, stage, nbuf, sums, parts,
+    ins, zs, zr, fs, fr, ns, yr, cs, nr, hs, hr, ls, os,
 ):
     frame = lax.axis_index("tm")
     group = lax.axis_index("head")
@@ -57,8 +57,6 @@
     has_next, has_prev = col < 15, col > 0
     from_prev = jnp.logical_and(z == 0, has_prev)
     from_next = jnp.logical_and(z == SIDE - 1, has_next)
-    next_dev = (col + 1) * SIDE
-    prev_dev = (col - 1) * SIDE + SIDE - 1
 
     loads = [pltpu.make_async_copy(q, q_in, ins.at[0]), pltpu.make_async_copy(k, k_in, ins.at[1])]
     loads += [pltpu.make_async_copy(v.at[:, cut(h)], zbuf.at[0, z, h], ins.at[2 + h]) for h in range(HEADS)]
@@ -75,31 +73,8 @@
     for j in range(1, GROUPS):
         greet({"head": (group + j) % GROUPS})
 
-    @pl.when(z > 0)
-    def _():
-        greet(tm(frame - 1))
-
-    @pl.when(z < SIDE - 1)
-    def _():
-        greet(tm(frame + 1))
-
-    @pl.when(has_next)
-    def _():
-        greet(tm(next_dev))
-
-    @pl.when(has_prev)
-    def _():
-        greet(tm(prev_dev))
-
-    @pl.when(from_prev)
-    def _():
-        for j in range(SIDE):
-            greet(tm((col - 1) * SIDE + j))
-
-    @pl.when(from_next)
-    def _():
-        for j in range(SIDE):
-            greet(tm((col + 1) * SIDE + j))
+    for j in range(1, SIDE):
+        greet(tm(col * SIDE + (z + j) % SIDE))
 
     loads[0].wait()
     loads[1].wait()
@@ -109,21 +84,9 @@
     both = jnp.where(lane == 0, q_part, jnp.where(lane == 1, k_part, 0.0))
     sums[...] = jnp.transpose(both)[:8]
 
-    lacks_near = jnp.logical_or(frame == 0, frame == FRAMES - 1)
-
-    @pl.when(lacks_near)
-    def _():
-        nbuf[...] = jnp.zeros_like(nbuf)
-
     for c in loads[2:]:
         c.wait()
-    greeted = PEERS + GROUPS - 1
-    for cond, n in (
-        (z > 0, 1), (z < SIDE - 1, 1), (has_next, 1), (has_prev, 1),
-        (from_prev, SIDE), (from_next, SIDE),
-    ):
-        greeted = greeted + jnp.where(cond, n, 0)
-    pl.semaphore_wait(barrier, greeted)
+    pl.semaphore_wait(barrier, PEERS + GROUPS - 1 + SIDE - 1)
 
     sum_copies = []
     for j in range(1, GROUPS):
@@ -133,18 +96,49 @@
         c.start()
         sum_copies.append(c)
 
-    def z_copy(t, j, hop, right):
+    def z_copy(t, j, hop, right, h=None):
         dev = frame + 1 if right else frame - 1
+        part = zbuf.at[t, j] if h is None else zbuf.at[t, j, h]
         return pltpu.make_async_remote_copy(
-            zbuf.at[t, j], zbuf.at[t, j], zs.at[int(right), hop, t], zr.at[j, t],
+            part, part, zs.at[int(right), hop, t], zr.at[j, t],
             device_id=tm(dev), device_id_type=MESH)
 
-    def near_copy(t, up):
-        part = pl.ds(2 * BLOCK * z, 2 * BLOCK)
+    quarter = pl.ds(2 * BLOCK * z, 2 * BLOCK)
+    over = (has_prev, has_next)
+    goal = (0, SIDE - 1)
+
+    def near_copy(t, up, h=None):
+        heads = slice(None) if h is None else h
         return pltpu.make_async_remote_copy(
-            zbuf.at[t, SIDE - 1 if up else 0, :, part], nbuf.at[t, :, part],
-            ns.at[int(up), t], nr.at[t],
-            device_id=tm(next_dev if up else prev_dev), device_id_type=MESH)
+            zbuf.at[t, SIDE - 1 if up else 0, heads, quarter], stage.at[1 - up, t, heads],
+            ns.at[up, t], yr.at[1 - up, t],
+            device_id=tm(frame + SIDE if up else frame - SIDE), device_id_type=MESH)
+
+    def cross(t):
+        for h in range(HEADS):
+            for up in (1, 0):
+                @pl.when(over[up])
+                def _():
+                    near_copy(t, up, h).start()
+
+    def last_copy(t, way):
+        return pltpu.make_async_remote_copy(
+            stage.at[way, t], nbuf.at[t, :, quarter], cs.at[way, t], nr.at[t],
+            device_id=tm(col * SIDE + goal[way]), device_id_type=MESH)
+
+    def deliver(t):
+        for way in (0, 1):
+            @pl.when(over[way])
+            def _():
+                pltpu.make_async_copy(stage.at[way, t], stage.at[way, t], yr.at[way, t]).wait()
+
+                @pl.when(z != goal[way])
+                def _():
+                    last_copy(t, way).start()
+
+                @pl.when(z == goal[way])
+                def _():
+                    pltpu.make_async_copy(stage.at[way, t], nbuf.at[t, :, quarter], nr.at[t]).start()
 
     def step_frame(s):
         if s == 0:
@@ -166,39 +160,23 @@
         part = out.at[s, t, pl.ds(half * HALF, HALF if half == 0 else PEERS - HALF)]
         return pltpu.make_async_copy(part, part, fs.at[s, t, half])
 
-    def column(s, t):
-        if s == 0:
-            @pl.when(z < SIDE - 1)
-            def _():
-                z_copy(t, z, 0, True).start()
-
-            @pl.when(z > 0)
-            def _():
-                z_copy(t, z, 0, False).start()
-        else:
-            @pl.when(z - s >= 0)
-            def _():
-                z_copy(t, z - s, s, True).wait_recv()
-
-                @pl.when(z < SIDE - 1)
-                def _():
-                    z_copy(t, z - s, s, True).start()
-
-            @pl.when(z + s < SIDE)
-            def _():
-                z_copy(t, z + s, s, False).wait_recv()
-
-                @pl.when(z > 0)
-                def _():
-                    z_copy(t, z + s, s, False).start()
-
-        @pl.when(jnp.logical_and(z == SIDE - 1 - s, has_next))
+    def arrive(s, t):
+        @pl.when(z - s >= 0)
         def _():
-            near_copy(t, True).start()
-
-        @pl.when(jnp.logical_and(z == s, has_prev))
+            z_copy(t, z - s, s, True).wait_recv()
+
+        @pl.when(z + s < SIDE)
         def _():
-            near_copy(t, False).start()
+            z_copy(t, z + s, s, False).wait_recv()
+
+    def column(s, t, h):
+        @pl.when(jnp.logical_and(z - s >= 0, z < SIDE - 1))
+        def _():
+            z_copy(t, z - s, s, True, h).start()
+
+        @pl.when(jnp.logical_and(z + s < SIDE, z > 0))
+        def _():
+            z_copy(t, z + s, s, False, h).start()
 
     def choose(s, t):
         j = step_frame(s)
@@ -221,13 +199,16 @@
         lax.fori_loop(0, HEADS, one_head, 0)
         pltpu.make_async_copy(own.at[t, j], far_o.at[t, g], ls.at[s, t]).start()
 
-    def post(s, t, half):
+    def post(s, t, half, beside=None):
         j = step_frame(s)
         for i in range(PEERS):
             if i // HALF == half:
                 far_copy(s, t, i, j).start()
-
-    column(0, 0)
+                if beside is not None and i % HALF < HEADS:
+                    column(*beside, i % HALF)
+
+    for h in range(HEADS):
+        column(0, 0, h)
     choose(0, 0)
     post(0, 0, 0)
     post(0, 0, 1)
@@ -240,11 +221,12 @@
     scale = lax.rsqrt(jnp.transpose(total) / FULL + epsilon)
     q_scale, k_scale = scale[:, 0:1], scale[:, 1:2]
     for h in range(HEADS):
-        k_norm = k_in[:, cut(h)].astype(jnp.float32) * k_scale * kg[:, cut(h)]
+        k_norm = k_in[:, cut(h)].astype(jnp.float32) * k_scale * kg[cut(h)].reshape(1, HEAD_DIM)
         zbuf[1, z, h] = k_norm.astype(jnp.bfloat16)
-    column(0, 1)
     for h in range(HEADS):
-        qn[h] = (q_in[:, cut(h)].astype(jnp.float32) * q_scale * qg[:, cut(h)]).astype(jnp.bfloat16)
+        column(0, 1, h)
+    for h in range(HEADS):
+        qn[h] = (q_in[:, cut(h)].astype(jnp.float32) * q_scale * qg[cut(h)].reshape(1, HEAD_DIM)).astype(jnp.bfloat16)
     q_out = pltpu.make_async_copy(qn, qn_o, os.at[0])
     q_out.start()
     order = [(s, t) for s in range(SIDE) for t in range(2)]
@@ -252,25 +234,25 @@
         s, t = order[r]
         choose(s, t)
         sent(*order[r - 1], 0).wait()
-        post(s, t, 0)
-        if r + 1 < len(order):
-            column(*order[r + 1])
+        beside = order[r + 1] if r + 1 < len(order) else None
+        if beside is not None:
+            arrive(*beside)
+        post(s, t, 0, beside if beside is not None and beside[0] < SIDE - 1 else None)
+        if r >= len(order) - 3 and r < len(order) - 1:
+            cross(r - (len(order) - 3))
+        if r == len(order) - 1:
+            deliver(0)
         sent(*order[r - 1], 1).wait()
         post(s, t, 1)
-
-    @pl.when(jnp.logical_or(from_prev, from_next))
-    def _():
-        for t in range(2):
-            pltpu.make_async_copy(nbuf.at[t], nbuf.at[t], nr.at[t]).wait()
+    deliver(1)
 
     def near_rows(t, h):
-        prev = jnp.where(z > 0, zbuf[t, jnp.maximum(z - 1, 0), h], nbuf[t, h])
-        after = jnp.where(z < SIDE - 1, zbuf[t, jnp.minimum(z + 1, SIDE - 1), h], nbuf[t, h])
-        return jnp.concatenate([prev, zbuf[t, z, h], after], axis=0)
+        return jnp.concatenate(
+            [zbuf[t, jnp.maximum(z - 1, 0), h], zbuf[t, z, h], zbuf[t, jnp.minimum(z + 1, SIDE - 1), h]], axis=0)
 
     place = lax.broadcasted_iota(jnp.int32, (1, NEARK), 1) // TOK
     near_ok = jnp.logical_and(
-        jnp.logical_or(place > 0, frame > 0), jnp.logical_or(place < 2, frame < FRAMES - 1))
+        jnp.logical_or(place > 0, z > 0), jnp.logical_or(place < 2, z < SIDE - 1))
     half_lane = lax.broadcasted_iota(jnp.int32, (ROWS, HEAD_DIM), 1) < BLOCK
 
     def near_tile(n, carry):
@@ -287,6 +269,27 @@
         return carry
 
     lax.fori_loop(0, HEADS * (TOK // ROWS), near_tile, 0)
+
+    def cross_tile(n, carry):
+        h, i = n // (TOK // ROWS), n % (TOK // ROWS)
+        rows = pl.ds(i * ROWS, ROWS)
+        score = lax.dot_general(qn[h, rows], nbuf[1, h], DIMS, preferred_element_type=jnp.float32)
+        old_peak, old_total = stat[h, rows][:, 0:1], stat[h, rows][:, BLOCK:BLOCK + 1]
+        peak = jnp.maximum(old_peak, score.max(-1, keepdims=True))
+        prob = jnp.exp2((score - peak) * RATE)
+        shrink = jnp.exp2((old_peak - peak) * RATE)
+        total = old_total * shrink + prob.sum(-1, keepdims=True)
+        acc[h, rows] = acc[h, rows] * shrink + jnp.dot(
+            prob.astype(jnp.bfloat16), nbuf[0, h], preferred_element_type=jnp.float32)
+        stat[h, rows] = jnp.where(half_lane, peak, total)
+        return carry
+
+    @pl.when(jnp.logical_or(from_prev, from_next))
+    def _():
+        for t in range(2):
+            pltpu.make_async_copy(nbuf.at[t], nbuf.at[t], nr.at[t]).wait()
+        lax.fori_loop(0, HEADS * (TOK // ROWS), cross_tile, 0)
+
     near_out = [pltpu.make_async_copy(acc, acc_o, os.at[1]), pltpu.make_async_copy(stat, stat_o, os.at[2])]
     for c in near_out:
         c.start()
@@ -304,13 +307,14 @@
             def _():
                 z_copy(t, z + s, s, False).wait_send()
 
-        @pl.when(has_next)
-        def _():
-            near_copy(t, True).wait_send()
-
-        @pl.when(has_prev)
-        def _():
-            near_copy(t, False).wait_send()
+        for way in (0, 1):
+            @pl.when(over[way])
+            def _():
+                near_copy(t, way).wait_send()
+
+            @pl.when(jnp.logical_and(over[way], z != goal[way]))
+            def _():
+                last_copy(t, way).wait_send()
     sent(*order[-1], 0).wait()
     sent(*order[-1], 1).wait()
     q_out.wait()
@@ -343,18 +347,19 @@
             pltpu.VMEM((2, SIDE) + heads, bf),
             pltpu.VMEM((SIDE, 2, PEERS, HEADS, BLOCK, HEAD_DIM), bf),
             pltpu.VMEM((2, SIDE, HEADS, BLOCK, HEAD_DIM), bf),
+            pltpu.VMEM((2, 2, HEADS, 2 * BLOCK, HEAD_DIM), bf),
             pltpu.VMEM((2,) + heads, bf),
             pltpu.VMEM((8, TOK), f32),
             pltpu.VMEM((GROUPS, 8, TOK), f32),
             dma((2 + HEADS,)),
             dma((2, SIDE, 2)), dma((SIDE, 2)),
             dma((SIDE, 2, 2)), dma((SIDE, 2)),
-            dma((2, 2)), dma((2,)),
+            dma((2, 2)), dma((2, 2)), dma((2, 2)), dma((2,)),
             dma((GROUPS,)), dma((GROUPS,)),
             dma((SIDE, 2)), dma((3,)),
         ],
         compiler_params=pltpu.CompilerParams(
-            collective_id=0, has_side_effects=True, vmem_limit_bytes=48 << 20),
+            collective_id=0, has_side_effects=True, vmem_limit_bytes=60 << 20),
     )(query, key, value, q_gain, k_gain, far_pick)
 
 
@@ -397,7 +402,7 @@
             ],
             out_specs=pl.BlockSpec((TOK, HEAD_DIM), lambda h, _: (0, h)),
         ),
-        compiler_params=pltpu.CompilerParams(vmem_limit_bytes=48 << 20),
+        compiler_params=pltpu.CompilerParams(vmem_limit_bytes=60 << 20),
     )(lists, q, acc, stat, far)
 
 
@@ -405,7 +410,7 @@
     frame = lax.axis_index("tm")
     mine = lax.dynamic_slice_in_dim(far_frames, frame * BLOCKS, BLOCKS, 0)
     held = spread(
-        query, key, value, q_gain.reshape(1, WIDTH), k_gain.reshape(1, WIDTH), far_pick)
+        query, key, value, q_gain, k_gain, far_pick)
     return attend(mine.reshape(-1), *held)
 
 

time: 202 us -> 182 us (0.901)
  the two profiles are of different devices: /device:TPU:252 before, /device:TPU:8 now
where the time goes in v3:
time: 182 us; the launch traced here: 181 us
  Pallas kernels  180 us (99%)
    pallas_call x1, Pallas kernels, spread(): pl.pallas_call(spread_kernel, out_shape=(jax.ShapeDtypeStruct(heads, bf),...  169 us
    pallas_call x1, Pallas kernels, attend(): pl.pallas_call(attend_kernel, out_shape=jax.ShapeDtypeStruct((TOK, WIDTH)...  11.1 us

profile of v3, /device:TPU:8, one launch (start us, length us, event | category | flops | bytes accessed | tf_op | source)
XLA Modules:
  0.0 181.3 jit_solution(13805467486726641082)
XLA Ops:
  0.0 0.0 copy-start
  0.0 0.8 copy-done
  0.8 0.1 constant_dynamic-slice_fusion
  0.8 0.1 copy.8
  0.9 0.7 reshape.3.lists
  1.6 168.5 %shard_map.73 = (bf16[5,512,128]{2,1,0:T(8,128)(2,1)}, f32[5,512,128]{2,1,0:T(8,128)}, f32[5,512,128]{2,1,0:T(8,128)}, bf16[2,64,5,64,128]{4,3,2,1,0:T(8,128)(2,1)}) custom-call(bf16[512,640]{1,0:T(8,128)(2,1)} %q.1, bf16[512,640]{1,0:T(8,128)(2,1)} %k.1, bf16[512,640]{1,0:T(8,128)(2,1)} %v.1, f32[640]{0:T(1024)} %qg.1, f32[640]{0:T(1024)} %kg.1, s32[64,64]{1,0:T(8,128)} %pick.1), custom_call_target="tpu_custom_call" | custom-call | tf_op jit(solution)/shard_map/pallas_call | solution.py:331
  170.1 11.1 %shard_map.74 = bf16[512,640]{1,0:T(8,128)(2,1)} custom-call(s32[96]{0:T(128)} %reshape.3.lists, bf16[5,512,128]{2,1,0:T(8,128)(2,1)} %get-tuple-element.9.q, f32[5,512,128]{2,1,0:T(8,128)} %get-tuple-element.10.acc, f32[5,512,128]{2,1,0:T(8,128)} %get-tuple-element.11.stat, bf16[2,64,5,64,128]{4,3,2,1,0:T(8,128)(2,1)} %get-tuple-element.12.far), custom_call_target="tpu_custom_call" | custom-call | tf_op jit(solution)/shard_map/pallas_call | solution.py:394
Async XLA Ops:
  0.0 0.8 copy-start

commit v4 on v3

--- a/solution.py
+++ b/solution.py
@@ -25,8 +25,8 @@
 masked = -1e30
 MESH = pl.DeviceIdType.MESH
 PLANE = (
-    (1, 0), (0, 1), (3, 0), (0, 3), (2, 0), (0, 2), (1, 1), (3, 3),
-    (1, 3), (3, 1), (2, 1), (1, 2), (2, 3), (3, 2), (2, 2),
+    (2, 2), (1, 1), (3, 3), (1, 3), (3, 1), (2, 1), (1, 2), (2, 3),
+    (3, 2), (2, 0), (0, 2), (1, 0), (0, 1), (3, 0), (0, 3),
 )
 PEERS = len(PLANE)
 HALF = 8
@@ -36,10 +36,11 @@
 
 
 def spread_kernel(
-    q, k, v, qg, kg, pick, qn_o, acc_o, stat_o, far_o,
-    q_in, k_in, qn, acc, stat, zbuf, out, own, stage, nbuf, sums, parts,
+    q, k, v, qg, kg, pick, lists, o,
+    q_in, k_in, qn, acc, stat, zbuf, out, own, stage, nbuf, sums, parts, far_v, far_k, weight, far_stat, o_heads,
     ins, zs, zr, fs, fr, ns, yr, cs, nr, hs, hr, ls, os,
 ):
+    far = (far_v, far_k)
     frame = lax.axis_index("tm")
     group = lax.axis_index("head")
     col, z = frame // SIDE, frame % SIDE
@@ -153,7 +154,7 @@
 
     def far_copy(s, t, i, j):
         return pltpu.make_async_remote_copy(
-            out.at[s, t, i], far_o.at[t, col * SIDE + j], fs.at[s, t, i // HALF], fr.at[s, t],
+            out.at[s, t, i], far[t].at[col * SIDE + j], fs.at[s, t, i // HALF], fr.at[s, t],
             device_id=tm(plane_peer(PLANE[i])), device_id_type=MESH)
 
     def sent(s, t, half):
@@ -197,7 +198,7 @@
             return carry
 
         lax.fori_loop(0, HEADS, one_head, 0)
-        pltpu.make_async_copy(own.at[t, j], far_o.at[t, g], ls.at[s, t]).start()
+        pltpu.make_async_copy(own.at[t, j], far[t].at[g], ls.at[s, t]).start()
 
     def post(s, t, half, beside=None):
         j = step_frame(s)
@@ -227,24 +228,28 @@
         column(0, 1, h)
     for h in range(HEADS):
         qn[h] = (q_in[:, cut(h)].astype(jnp.float32) * q_scale * qg[cut(h)].reshape(1, HEAD_DIM)).astype(jnp.bfloat16)
-    q_out = pltpu.make_async_copy(qn, qn_o, os.at[0])
-    q_out.start()
-    order = [(s, t) for s in range(SIDE) for t in range(2)]
+    order = [(0, 0), (0, 1), (1, 0), (1, 1), (2, 1), (2, 0), (3, 1), (3, 0)]
     for r in range(1, len(order)):
         s, t = order[r]
+        beside = order[r + 1] if r + 1 < len(order) else None
+        moves = beside is not None and beside[0] < SIDE - 1
+        early = beside != (2, 1)
         choose(s, t)
         sent(*order[r - 1], 0).wait()
-        beside = order[r + 1] if r + 1 < len(order) else None
-        if beside is not None:
+        if beside is not None and early:
             arrive(*beside)
-        post(s, t, 0, beside if beside is not None and beside[0] < SIDE - 1 else None)
-        if r >= len(order) - 3 and r < len(order) - 1:
-            cross(r - (len(order) - 3))
-        if r == len(order) - 1:
-            deliver(0)
+        post(s, t, 0, beside if moves and early else None)
+        if beside is not None and not early:
+            arrive(*beside)
+        if r == 5:
+            cross(1)
+        if r == 6:
+            cross(0)
+        if r == 7:
+            deliver(1)
         sent(*order[r - 1], 1).wait()
-        post(s, t, 1)
-    deliver(1)
+        post(s, t, 1, beside if moves and not early else None)
+    deliver(0)
 
     def near_rows(t, h):
         return jnp.concatenate(
@@ -269,6 +274,34 @@
         return carry
 
     lax.fori_loop(0, HEADS * (TOK // ROWS), near_tile, 0)
+
+    def arrived(t):
+        for s in range(SIDE):
+            pltpu.make_async_copy(own.at[t, 0], far[t].at[0], ls.at[s, t]).wait()
+            pltpu.make_async_copy(out.at[s, t], out.at[s, t], fr.at[s, t]).wait()
+
+    slot = lax.broadcasted_iota(jnp.int32, (1, FARK), 1) // BLOCK
+
+    def far_scores(h, carry):
+        scores = []
+        for b in range(BLOCKS):
+            sources = [lists[b * NFAR + n] for n in SLOTS]
+            bias = jnp.zeros((1, FARK), jnp.float32)
+            for n, g in enumerate(sources):
+                bias = jnp.where(slot == n, jnp.where(g >= 0, 0.0, masked), bias)
+            keys = jnp.concatenate([far_k[jnp.maximum(g, 0), h] for g in sources], axis=0)
+            scores.append(lax.dot_general(
+                qn[h, b * BLOCK:(b + 1) * BLOCK], keys, DIMS, preferred_element_type=jnp.float32) + bias)
+        for b in range(BLOCKS):
+            peak = scores[b].max(-1, keepdims=True)
+            prob = jnp.exp2((scores[b] - peak) * RATE)
+            weight[h, b] = prob.astype(jnp.bfloat16)
+            far_stat[h, b * BLOCK:(b + 1) * BLOCK] = jnp.where(
+                half_lane[:BLOCK], peak, prob.sum(-1, keepdims=True))
+        return carry
+
+    arrived(1)
+    lax.fori_loop(0, HEADS, far_scores, 0)
 
     def cross_tile(n, carry):
         h, i = n // (TOK // ROWS), n % (TOK // ROWS)
@@ -290,15 +323,30 @@
             pltpu.make_async_copy(nbuf.at[t], nbuf.at[t], nr.at[t]).wait()
         lax.fori_loop(0, HEADS * (TOK // ROWS), cross_tile, 0)
 
-    near_out = [pltpu.make_async_copy(acc, acc_o, os.at[1]), pltpu.make_async_copy(stat, stat_o, os.at[2])]
-    for c in near_out:
-        c.start()
+    def o_copy(h):
+        cols = pl.ds(pl.multiple_of(h * HEAD_DIM, HEAD_DIM), HEAD_DIM)
+        return pltpu.make_async_copy(o_heads.at[h], o.at[:, cols], os.at[h])
+
+    def far_values(h, carry):
+        for b in range(BLOCKS):
+            rows = slice(b * BLOCK, (b + 1) * BLOCK)
+            vals = jnp.concatenate(
+                [far_v[jnp.maximum(lists[b * NFAR + n], 0), h] for n in SLOTS], axis=0)
+            near_peak, near_total = stat[h, rows][:, 0:1], stat[h, rows][:, BLOCK:BLOCK + 1]
+            far_peak, far_total = far_stat[h, rows][:, 0:1], far_stat[h, rows][:, BLOCK:BLOCK + 1]
+            peak = jnp.maximum(near_peak, far_peak)
+            a = jnp.exp2((near_peak - peak) * RATE)
+            c = jnp.exp2((far_peak - peak) * RATE)
+            mixed = acc[h, rows] * a + jnp.dot(weight[h, b], vals, preferred_element_type=jnp.float32) * c
+            o_heads[h, rows] = (mixed / (near_total * a + far_total * c)).astype(jnp.bfloat16)
+        o_copy(h).start()
+        return carry
+
+    arrived(0)
+    lax.fori_loop(0, HEADS, far_values, 0)
 
     for t in range(2):
         for s in range(SIDE):
-            pltpu.make_async_copy(own.at[t, 0], far_o.at[t, 0], ls.at[s, t]).wait()
-            pltpu.make_async_copy(out.at[s, t], out.at[s, t], fr.at[s, t]).wait()
-
             @pl.when(jnp.logical_and(z - s >= 0, z < SIDE - 1))
             def _():
                 z_copy(t, z - s, s, True).wait_send()
@@ -317,27 +365,23 @@
                 last_copy(t, way).wait_send()
     sent(*order[-1], 0).wait()
     sent(*order[-1], 1).wait()
-    q_out.wait()
-    for c in near_out:
-        c.wait()
-
-
-def spread(query, key, value, q_gain, k_gain, far_pick):
+    for h in range(HEADS):
+        o_copy(h).wait()
+
+
+def spread(query, key, value, q_gain, k_gain, far_pick, lists):
     vmem = pl.BlockSpec(memory_space=pltpu.VMEM)
     hbm = pl.BlockSpec(memory_space=pl.ANY)
+    smem = pl.BlockSpec(memory_space=pltpu.SMEM)
     dma = pltpu.SemaphoreType.DMA
     bf, f32 = jnp.bfloat16, jnp.float32
     heads = (HEADS, TOK, HEAD_DIM)
+    far = (FRAMES, HEADS, BLOCK, HEAD_DIM)
     return pl.pallas_call(
         spread_kernel,
-        out_shape=(
-            jax.ShapeDtypeStruct(heads, bf),
-            jax.ShapeDtypeStruct(heads, f32),
-            jax.ShapeDtypeStruct(heads, f32),
-            jax.ShapeDtypeStruct((2, FRAMES, HEADS, BLOCK, HEAD_DIM), bf),
-        ),
-        in_specs=[hbm] * 3 + [vmem] * 2 + [pl.BlockSpec(memory_space=pltpu.SMEM)],
-        out_specs=(hbm,) * 4,
+        out_shape=jax.ShapeDtypeStruct((TOK, WIDTH), bf),
+        in_specs=[hbm] * 3 + [vmem] * 2 + [smem] * 2,
+        out_specs=hbm,
         scratch_shapes=[
             pltpu.VMEM((TOK, WIDTH), bf),
             pltpu.VMEM((TOK, WIDTH), bf),
@@ -351,67 +395,27 @@
             pltpu.VMEM((2,) + heads, bf),
             pltpu.VMEM((8, TOK), f32),
             pltpu.VMEM((GROUPS, 8, TOK), f32),
+            pltpu.VMEM(far, bf),
+            pltpu.VMEM(far, bf),
+            pltpu.VMEM((HEADS, BLOCKS, BLOCK, FARK), bf),
+            pltpu.VMEM(heads, f32),
+            pltpu.VMEM(heads, bf),
             dma((2 + HEADS,)),
             dma((2, SIDE, 2)), dma((SIDE, 2)),
             dma((SIDE, 2, 2)), dma((SIDE, 2)),
             dma((2, 2)), dma((2, 2)), dma((2, 2)), dma((2,)),
             dma((GROUPS,)), dma((GROUPS,)),
-            dma((SIDE, 2)), dma((3,)),
+            dma((SIDE, 2)), dma((HEADS,)),
         ],
         compiler_params=pltpu.CompilerParams(
             collective_id=0, has_side_effects=True, vmem_limit_bytes=60 << 20),
-    )(query, key, value, q_gain, k_gain, far_pick)
-
-
-def attend_kernel(lists, q, acc, stat, far, o):
-    slot = lax.broadcasted_iota(jnp.int32, (1, FARK), 1) // BLOCK
-    scores, picked = [], []
-    for b in range(BLOCKS):
-        sources = [lists[b * NFAR + s] for s in SLOTS]
-        bias = jnp.zeros((1, FARK), jnp.float32)
-        for i, g in enumerate(sources):
-            bias = jnp.where(slot == i, jnp.where(g >= 0, 0.0, masked), bias)
-        held = [jnp.maximum(g, 0) for g in sources]
-        far_k = jnp.concatenate([far[1, g, 0] for g in held], axis=0)
-        picked.append(held)
-        scores.append(lax.dot_general(
-            q[0, b * BLOCK:(b + 1) * BLOCK], far_k, DIMS, preferred_element_type=jnp.float32) + bias)
-    for b in range(BLOCKS):
-        rows = slice(b * BLOCK, (b + 1) * BLOCK)
-        near_peak, near_total = stat[0, rows, 0:1], stat[0, rows, BLOCK:BLOCK + 1]
-        peak = jnp.maximum(near_peak, scores[b].max(-1, keepdims=True))
-        prob = jnp.exp2((scores[b] - peak) * RATE)
-        shrink = jnp.exp2((near_peak - peak) * RATE)
-        total = near_total * shrink + prob.sum(-1, keepdims=True)
-        far_v = jnp.concatenate([far[0, g, 0] for g in picked[b]], axis=0)
-        sums = acc[0, rows] * shrink + jnp.dot(
-            prob.astype(jnp.bfloat16), far_v, preferred_element_type=jnp.float32)
-        o[rows] = (sums / total).astype(jnp.bfloat16)
-
-
-def attend(lists, q, acc, stat, far):
-    head = pl.BlockSpec((1, TOK, HEAD_DIM), lambda h, _: (h, 0, 0))
-    return pl.pallas_call(
-        attend_kernel,
-        out_shape=jax.ShapeDtypeStruct((TOK, WIDTH), jnp.bfloat16),
-        grid_spec=pltpu.PrefetchScalarGridSpec(
-            num_scalar_prefetch=1,
-            grid=(HEADS,),
-            in_specs=[head] * 3 + [
-                pl.BlockSpec((2, FRAMES, 1, BLOCK, HEAD_DIM), lambda h, _: (0, 0, h, 0, 0)),
-            ],
-            out_specs=pl.BlockSpec((TOK, HEAD_DIM), lambda h, _: (0, h)),
-        ),
-        compiler_params=pltpu.CompilerParams(vmem_limit_bytes=60 << 20),
-    )(lists, q, acc, stat, far)
+    )(query, key, value, q_gain, k_gain, far_pick, lists)
 
 
 def local(query, key, value, q_gain, k_gain, far_frames, far_pick):
     frame = lax.axis_index("tm")
     mine = lax.dynamic_slice_in_dim(far_frames, frame * BLOCKS, BLOCKS, 0)
-    held = spread(
-        query, key, value, q_gain, k_gain, far_pick)
-    return attend(mine.reshape(-1), *held)
+    return spread(query, key, value, q_gain, k_gain, far_pick, mine.reshape(-1))
 
 
 def solution(mesh):

time: 182 us -> 180 us (0.989)
  the two profiles are of different devices: /device:TPU:8 before, /device:TPU:2 now
where the time goes in v4:
time: 180 us
  Pallas kernels  176 us (98%)
  local copies, waits for them, and re-layouts  3.49 us (2%)
    pallas_call x1, Pallas kernels, spread(): pl.pallas_call(spread_kernel, out_shape=jax.ShapeDtypeStruct((TOK, WIDTH)...  176 us

profile of v4, /device:TPU:2, one launch (start us, length us, event | category | flops | bytes accessed | tf_op | source)
XLA Modules:
  0.0 179.6 jit_solution(4001362710079590272)
XLA Ops:
  0.0 0.0 copy-start
  0.0 0.8 copy-done
  0.8 0.1 constant_dynamic-slice_fusion
  0.8 0.1 copy.8
  0.9 0.6 reshape.3.lists
  1.5 176.1 %shard_map.73 = bf16[512,640]{1,0:T(8,128)(2,1)} custom-call(bf16[512,640]{1,0:T(8,128)(2,1)} %q.1, bf16[512,640]{1,0:T(8,128)(2,1)} %k.1, bf16[512,640]{1,0:T(8,128)(2,1)} %v.1, f32[640]{0:T(1024)} %qg.1, f32[640]{0:T(1024)} %kg.1, s32[64,64]{1,0:T(8,128)} %pick.1, s32[96]{0:T(128)} %reshape.3.lists), custom_call_target="tpu_custom_call" | custom-call | tf_op jit(solution)/shard_map/pallas_call | solution.py:380
  177.7 2.0 %copy.10 = bf16[512,640]{1,0:T(8,128)(2,1)} copy(bf16[512,640]{1,0:T(8,128)(2,1)} %shard_map.73) | data formatting | bytes 1310720
Async XLA Ops:
  0.0 0.8 copy-start

commit v5 on v4

--- a/solution.py
+++ b/solution.py
@@ -25,8 +25,8 @@
 masked = -1e30
 MESH = pl.DeviceIdType.MESH
 PLANE = (
-    (2, 2), (1, 1), (3, 3), (1, 3), (3, 1), (2, 1), (1, 2), (2, 3),
-    (3, 2), (2, 0), (0, 2), (1, 0), (0, 1), (3, 0), (0, 3),
+    (2, 2), (2, 1), (1, 2), (2, 3), (3, 2), (1, 1), (3, 3), (1, 3),
+    (3, 1), (2, 0), (0, 2), (1, 0), (0, 1), (3, 0), (0, 3),
 )
 PEERS = len(PLANE)
 HALF = 8
@@ -115,10 +115,12 @@
             ns.at[up, t], yr.at[1 - up, t],
             device_id=tm(frame + SIDE if up else frame - SIDE), device_id_type=MESH)
 
-    def cross(t):
+    def cross(t, late):
         for h in range(HEADS):
             for up in (1, 0):
-                @pl.when(over[up])
+                outer = z == (0 if up else SIDE - 1)
+
+                @pl.when(jnp.logical_and(over[up], outer if late else jnp.logical_not(outer)))
                 def _():
                     near_copy(t, up, h).start()
 
@@ -228,29 +230,6 @@
         column(0, 1, h)
     for h in range(HEADS):
         qn[h] = (q_in[:, cut(h)].astype(jnp.float32) * q_scale * qg[cut(h)].reshape(1, HEAD_DIM)).astype(jnp.bfloat16)
-    order = [(0, 0), (0, 1), (1, 0), (1, 1), (2, 1), (2, 0), (3, 1), (3, 0)]
-    for r in range(1, len(order)):
-        s, t = order[r]
-        beside = order[r + 1] if r + 1 < len(order) else None
-        moves = beside is not None and beside[0] < SIDE - 1
-        early = beside != (2, 1)
-        choose(s, t)
-        sent(*order[r - 1], 0).wait()
-        if beside is not None and early:
-            arrive(*beside)
-        post(s, t, 0, beside if moves and early else None)
-        if beside is not None and not early:
-            arrive(*beside)
-        if r == 5:
-            cross(1)
-        if r == 6:
-            cross(0)
-        if r == 7:
-            deliver(1)
-        sent(*order[r - 1], 1).wait()
-        post(s, t, 1, beside if moves and not early else None)
-    deliver(0)
-
     def near_rows(t, h):
         return jnp.concatenate(
             [zbuf[t, jnp.maximum(z - 1, 0), h], zbuf[t, z, h], zbuf[t, jnp.minimum(z + 1, SIDE - 1), h]], axis=0)
@@ -273,7 +252,31 @@
         stat[h, rows] = jnp.where(half_lane, peak, total)
         return carry
 
-    lax.fori_loop(0, HEADS * (TOK // ROWS), near_tile, 0)
+    order = [(0, 0), (0, 1), (1, 0), (1, 1), (2, 1), (2, 0), (3, 1), (3, 0)]
+    for r in range(1, len(order)):
+        s, t = order[r]
+        beside = order[r + 1] if r + 1 < len(order) else None
+        moves = beside is not None and beside[0] < SIDE - 1
+        early = beside != (2, 1)
+        choose(s, t)
+        if beside is not None and early:
+            arrive(*beside)
+        post(s, t, 0, beside if moves and early else None)
+        if beside is not None and not early:
+            arrive(*beside)
+        if r == 4:
+            cross(1, False)
+            cross(0, False)
+        if r == 5:
+            cross(1, True)
+        if r == 6:
+            cross(0, True)
+        if r == 7:
+            deliver(1)
+        post(s, t, 1, beside if moves and not early else None)
+        if r == 7:
+            lax.fori_loop(0, HEADS * (TOK // ROWS), near_tile, 0)
+    deliver(0)
 
     def arrived(t):
         for s in range(SIDE):
@@ -363,8 +366,9 @@
             @pl.when(jnp.logical_and(over[way], z != goal[way]))
             def _():
                 last_copy(t, way).wait_send()
-    sent(*order[-1], 0).wait()
-    sent(*order[-1], 1).wait()
+    for st in order:
+        sent(*st, 0).wait()
+        sent(*st, 1).wait()
     for h in range(HEADS):
         o_copy(h).wait()
 

time: 180 us -> 172 us (0.956)
  Pallas kernels: 176 us -> 168 us
    pallas_call x1, Pallas kernels: 176 us -> 168 us  [spread(): pl.pallas_call(spread_kernel, out_shape=jax.ShapeDtypeStruct((TOK, WIDTH)...]
where the time goes in v5:
time: 172 us
  Pallas kernels  168 us (98%)
  local copies, waits for them, and re-layouts  3.49 us (2%)
    pallas_call x1, Pallas kernels, spread(): pl.pallas_call(spread_kernel, out_shape=jax.ShapeDtypeStruct((TOK, WIDTH)...  168 us

profile of v5, /device:TPU:2, one launch (start us, length us, event | category | flops | bytes accessed | tf_op | source)
XLA Modules:
  0.0 171.8 jit_solution(9443415866950799919)
XLA Ops:
  0.0 0.0 copy-start
  0.0 0.8 copy-done
  0.8 0.1 constant_dynamic-slice_fusion
  0.8 0.1 copy.8
  0.9 0.6 reshape.3.lists
  1.5 168.3 %shard_map.73 = bf16[512,640]{1,0:T(8,128)(2,1)} custom-call(bf16[512,640]{1,0:T(8,128)(2,1)} %q.1, bf16[512,640]{1,0:T(8,128)(2,1)} %k.1, bf16[512,640]{1,0:T(8,128)(2,1)} %v.1, f32[640]{0:T(1024)} %qg.1, f32[640]{0:T(1024)} %kg.1, s32[64,64]{1,0:T(8,128)} %pick.1, s32[96]{0:T(128)} %reshape.3.lists), custom_call_target="tpu_custom_call" | custom-call | tf_op jit(solution)/shard_map/pallas_call | solution.py:384
  169.8 2.0 %copy.10 = bf16[512,640]{1,0:T(8,128)(2,1)} copy(bf16[512,640]{1,0:T(8,128)(2,1)} %shard_map.73) | data formatting | bytes 1310720
Async XLA Ops:
  0.0 0.8 copy-start

commit v6 on v5

--- a/solution.py
+++ b/solution.py
@@ -303,9 +303,6 @@
                 half_lane[:BLOCK], peak, prob.sum(-1, keepdims=True))
         return carry
 
-    arrived(1)
-    lax.fori_loop(0, HEADS, far_scores, 0)
-
     def cross_tile(n, carry):
         h, i = n // (TOK // ROWS), n % (TOK // ROWS)
         rows = pl.ds(i * ROWS, ROWS)
@@ -326,6 +323,22 @@
             pltpu.make_async_copy(nbuf.at[t], nbuf.at[t], nr.at[t]).wait()
         lax.fori_loop(0, HEADS * (TOK // ROWS), cross_tile, 0)
 
+    arrived(1)
+    lax.fori_loop(0, HEADS, far_scores, 0)
+
+    def factors(h, carry):
+        near_peak, near_total = stat[h][:, 0:1], stat[h][:, BLOCK:BLOCK + 1]
+        far_peak, far_total = far_stat[h][:, 0:1], far_stat[h][:, BLOCK:BLOCK + 1]
+        peak = jnp.maximum(near_peak, far_peak)
+        a = jnp.exp2((near_peak - peak) * RATE)
+        c = jnp.exp2((far_peak - peak) * RATE)
+        share = 1.0 / (near_total * a + far_total * c)
+        acc[h] = acc[h] * (a * share)
+        far_stat[h] = jnp.broadcast_to(c * share, (TOK, HEAD_DIM))
+        return carry
+
+    lax.fori_loop(0, HEADS, factors, 0)
+
     def o_copy(h):
         cols = pl.ds(pl.multiple_of(h * HEAD_DIM, HEAD_DIM), HEAD_DIM)
         return pltpu.make_async_copy(o_heads.at[h], o.at[:, cols], os.at[h])
@@ -335,13 +348,8 @@
             rows = slice(b * BLOCK, (b + 1) * BLOCK)
             vals = jnp.concatenate(
                 [far_v[jnp.maximum(lists[b * NFAR + n], 0), h] for n in SLOTS], axis=0)
-            near_peak, near_total = stat[h, rows][:, 0:1], stat[h, rows][:, BLOCK:BLOCK + 1]
-            far_peak, far_total = far_stat[h, rows][:, 0:1], far_stat[h, rows][:, BLOCK:BLOCK + 1]
-            peak = jnp.maximum(near_peak, far_peak)
-            a = jnp.exp2((near_peak - peak) * RATE)
-            c = jnp.exp2((far_peak - peak) * RATE)
-            mixed = acc[h, rows] * a + jnp.dot(weight[h, b], vals, preferred_element_type=jnp.float32) * c
-            o_heads[h, rows] = (mixed / (near_total * a + far_total * c)).astype(jnp.bfloat16)
+            far_out = jnp.dot(weight[h, b], vals, preferred_element_type=jnp.float32)
+            o_heads[h, rows] = (acc[h, rows] + far_out * far_stat[h, rows]).astype(jnp.bfloat16)
         o_copy(h).start()
         return carry
 

time: 172 us -> 169 us (0.983)
  the two profiles are of different devices: /device:TPU:2 before, /device:TPU:122 now
where the time goes in v6:
time: 169 us
  Pallas kernels  165 us (98%)
  local copies, waits for them, and re-layouts  3.49 us (2%)
    pallas_call x1, Pallas kernels, spread(): pl.pallas_call(spread_kernel, out_shape=jax.ShapeDtypeStruct((TOK, WIDTH)...  165 us

profile of v6, /device:TPU:122, one launch (start us, length us, event | category | flops | bytes accessed | tf_op | source)
XLA Modules:
  0.0 169.0 jit_solution(6153859331987403360)
XLA Ops:
  0.0 0.0 copy-start
  0.0 0.8 copy-done
  0.8 0.1 constant_dynamic-slice_fusion
  0.8 0.1 copy.8
  0.9 0.6 reshape.3.lists
  1.5 165.5 %shard_map.73 = bf16[512,640]{1,0:T(8,128)(2,1)} custom-call(bf16[512,640]{1,0:T(8,128)(2,1)} %q.1, bf16[512,640]{1,0:T(8,128)(2,1)} %k.1, bf16[512,640]{1,0:T(8,128)(2,1)} %v.1, f32[640]{0:T(1024)} %qg.1, f32[640]{0:T(1024)} %kg.1, s32[64,64]{1,0:T(8,128)} %pick.1, s32[96]{0:T(128)} %reshape.3.lists), custom_call_target="tpu_custom_call" | custom-call | tf_op jit(solution)/shard_map/pallas_call | solution.py:392
  167.0 2.0 %copy.10 = bf16[512,640]{1,0:T(8,128)(2,1)} copy(bf16[512,640]{1,0:T(8,128)(2,1)} %shard_map.73) | data formatting | bytes 1310720
Async XLA Ops:
  0.0 0.8 copy-start

commit v7 on v6

--- a/solution.py
+++ b/solution.py
@@ -29,7 +29,6 @@
     (3, 1), (2, 0), (0, 2), (1, 0), (0, 1), (3, 0), (0, 3),
 )
 PEERS = len(PLANE)
-HALF = 8
 ROWS = 256
 RATE = HEAD_DIM ** (-0.5) * 1.4426950408889634
 DIMS = (((1,), (1,)), ((), ()))
@@ -37,10 +36,10 @@
 
 def spread_kernel(
     q, k, v, qg, kg, pick, lists, o,
-    q_in, k_in, qn, acc, stat, zbuf, out, own, stage, nbuf, sums, parts, far_v, far_k, weight, far_stat, o_heads,
+    q_in, k_in, qn, acc, stat, zbuf, out, own, stage, nbuf, sums, parts, far_va, far_vb, far_k, weight, far_stat, o_heads,
     ins, zs, zr, fs, fr, ns, yr, cs, nr, hs, hr, ls, os,
 ):
-    far = (far_v, far_k)
+    parts_of = (pl.ds(0, 3), pl.ds(3, HEADS - 3))
     frame = lax.axis_index("tm")
     group = lax.axis_index("head")
     col, z = frame // SIDE, frame % SIDE
@@ -154,14 +153,21 @@
             r = jnp.where(z == i, table[i], r)
         return r
 
-    def far_copy(s, t, i, j):
+    def landing(t, part, g):
+        return (far_va, far_vb)[part].at[g] if t == 0 else far_k.at[g, parts_of[part]]
+
+    def far_copy(s, t, i, j, part):
         return pltpu.make_async_remote_copy(
-            out.at[s, t, i], far[t].at[col * SIDE + j], fs.at[s, t, i // HALF], fr.at[s, t],
+            out.at[s, t, i, parts_of[part]], landing(t, part, col * SIDE + j),
+            fs.at[s, t, part], fr.at[s, t, part],
             device_id=tm(plane_peer(PLANE[i])), device_id_type=MESH)
 
-    def sent(s, t, half):
-        part = out.at[s, t, pl.ds(half * HALF, HALF if half == 0 else PEERS - HALF)]
-        return pltpu.make_async_copy(part, part, fs.at[s, t, half])
+    def own_copy(s, t, part, j, g):
+        return pltpu.make_async_copy(own.at[t, j, parts_of[part]], landing(t, part, g), ls.at[s, t, part])
+
+    def sent(s, t, part):
+        held = out.at[s, t, :, parts_of[part]]
+        return pltpu.make_async_copy(held, held, fs.at[s, t, part])
 
     def arrive(s, t):
         @pl.when(z - s >= 0)
@@ -200,15 +206,15 @@
             return carry
 
         lax.fori_loop(0, HEADS, one_head, 0)
-        pltpu.make_async_copy(own.at[t, j], far[t].at[g], ls.at[s, t]).start()
-
-    def post(s, t, half, beside=None):
+        for part in (0, 1):
+            own_copy(s, t, part, j, g).start()
+
+    def post(s, t, part, beside=None):
         j = step_frame(s)
         for i in range(PEERS):
-            if i // HALF == half:
-                far_copy(s, t, i, j).start()
-                if beside is not None and i % HALF < HEADS:
-                    column(*beside, i % HALF)
+            far_copy(s, t, i, j, part).start()
+            if beside is not None and i % 3 == 0:
+                column(*beside, i // 3)
 
     for h in range(HEADS):
         column(0, 0, h)
@@ -278,10 +284,11 @@
             lax.fori_loop(0, HEADS * (TOK // ROWS), near_tile, 0)
     deliver(0)
 
-    def arrived(t):
+    def arrived(t, part):
         for s in range(SIDE):
-            pltpu.make_async_copy(own.at[t, 0], far[t].at[0], ls.at[s, t]).wait()
-            pltpu.make_async_copy(out.at[s, t], out.at[s, t], fr.at[s, t]).wait()
+            own_copy(s, t, part, 0, 0).wait()
+            held = out.at[s, t, :, parts_of[part]]
+            pltpu.make_async_copy(held, held, fr.at[s, t, part]).wait()
 
     slot = lax.broadcasted_iota(jnp.int32, (1, FARK), 1) // BLOCK
 
@@ -323,7 +330,8 @@
             pltpu.make_async_copy(nbuf.at[t], nbuf.at[t], nr.at[t]).wait()
         lax.fori_loop(0, HEADS * (TOK // ROWS), cross_tile, 0)
 
-    arrived(1)
+    arrived(1, 0)
+    arrived(1, 1)
     lax.fori_loop(0, HEADS, far_scores, 0)
 
     def factors(h, carry):
@@ -343,18 +351,20 @@
         cols = pl.ds(pl.multiple_of(h * HEAD_DIM, HEAD_DIM), HEAD_DIM)
         return pltpu.make_async_copy(o_heads.at[h], o.at[:, cols], os.at[h])
 
-    def far_values(h, carry):
+    def far_values(held, first, h, carry):
         for b in range(BLOCKS):
             rows = slice(b * BLOCK, (b + 1) * BLOCK)
             vals = jnp.concatenate(
-                [far_v[jnp.maximum(lists[b * NFAR + n], 0), h] for n in SLOTS], axis=0)
+                [held[jnp.maximum(lists[b * NFAR + n], 0), h - first] for n in SLOTS], axis=0)
             far_out = jnp.dot(weight[h, b], vals, preferred_element_type=jnp.float32)
             o_heads[h, rows] = (acc[h, rows] + far_out * far_stat[h, rows]).astype(jnp.bfloat16)
         o_copy(h).start()
         return carry
 
-    arrived(0)
-    lax.fori_loop(0, HEADS, far_values, 0)
+    arrived(0, 0)
+    lax.fori_loop(0, 3, functools.partial(far_values, far_va, 0), 0)
+    arrived(0, 1)
+    lax.fori_loop(3, HEADS, functools.partial(far_values, far_vb, 3), 0)
 
     for t in range(2):
         for s in range(SIDE):
@@ -407,17 +417,18 @@
             pltpu.VMEM((2,) + heads, bf),
             pltpu.VMEM((8, TOK), f32),
             pltpu.VMEM((GROUPS, 8, TOK), f32),
-            pltpu.VMEM(far, bf),
+            pltpu.VMEM((FRAMES, 3, BLOCK, HEAD_DIM), bf),
+            pltpu.VMEM((FRAMES, HEADS - 3, BLOCK, HEAD_DIM), bf),
             pltpu.VMEM(far, bf),
             pltpu.VMEM((HEADS, BLOCKS, BLOCK, FARK), bf),
             pltpu.VMEM(heads, f32),
             pltpu.VMEM(heads, bf),
             dma((2 + HEADS,)),
             dma((2, SIDE, 2)), dma((SIDE, 2)),
-            dma((SIDE, 2, 2)), dma((SIDE, 2)),
+            dma((SIDE, 2, 2)), dma((SIDE, 2, 2)),
             dma((2, 2)), dma((2, 2)), dma((2, 2)), dma((2,)),
             dma((GROUPS,)), dma((GROUPS,)),
-            dma((SIDE, 2)), dma((HEADS,)),
+            dma((SIDE, 2, 2)), dma((HEADS,)),
         ],
         compiler_params=pltpu.CompilerParams(
             collective_id=0, has_side_effects=True, vmem_limit_bytes=60 << 20),

time: 169 us -> 170 us (level)
  no operation moved by 1% of the time
where the time goes in v7:
time: 170 us
  Pallas kernels  166 us (98%)
  local copies, waits for them, and re-layouts  3.49 us (2%)
    pallas_call x1, Pallas kernels, spread(): pl.pallas_call(spread_kernel, out_shape=jax.ShapeDtypeStruct((TOK, WIDTH)...  166 us

profile of v7, /device:TPU:122, one launch (start us, length us, event | category | flops | bytes accessed | tf_op | source)
XLA Modules:
  0.0 169.6 jit_solution(14112954054956919951)
XLA Ops:
  0.0 0.0 copy-start
  0.0 0.8 copy-done
  0.8 0.1 constant_dynamic-slice_fusion
  0.8 0.1 copy.8
  0.9 0.6 reshape.3.lists
  1.5 166.1 %shard_map.73 = bf16[512,640]{1,0:T(8,128)(2,1)} custom-call(bf16[512,640]{1,0:T(8,128)(2,1)} %q.1, bf16[512,640]{1,0:T(8,128)(2,1)} %k.1, bf16[512,640]{1,0:T(8,128)(2,1)} %v.1, f32[640]{0:T(1024)} %qg.1, f32[640]{0:T(1024)} %kg.1, s32[64,64]{1,0:T(8,128)} %pick.1, s32[96]{0:T(128)} %reshape.3.lists), custom_call_target="tpu_custom_call" | custom-call | tf_op jit(solution)/shard_map/pallas_call | solution.py:402
  167.6 2.0 %copy.10 = bf16[512,640]{1,0:T(8,128)(2,1)} copy(bf16[512,640]{1,0:T(8,128)(2,1)} %shard_map.73) | data formatting | bytes 1310720
Async XLA Ops:
  0.0 0.8 copy-start
